TPU v7x, 256 devices: a whole 4x4x8 slice. The times are simulated.
256 devices in a mesh: lat: 8 (over y, x_hi), lon: 32 (over x_lo, z, core).
Axes of the slice: x: 4 (x_hi: 2, x_lo: 2; x = x_hi * 2 + x_lo), y: 4, z: 8, core: 2. Of those that a mesh axis runs over, the one named last changes fastest.
Arguments:
- tokens: bfloat16 [4, 48, 768, 512], P(None, 'lat', 'lon'), may hold values from -6 to 6
- cotangent: bfloat16 [4, 48, 768, 512], P(None, 'lat', 'lon'), may hold values from -6 to 6
- w_qkv: bfloat16 [512, 1536], replicated, may hold values from -0.26516504 to 0.26516504
- w_out: bfloat16 [512, 512], replicated, may hold values from -0.25 to 0.25
- norm_gain_vector: float32 [512], replicated, may hold values from 0.1 to 1.9
Outputs:
- layer_out: bfloat16 [4, 48, 768, 512], P(None, 'lat', 'lon')
- grad_tokens: bfloat16 [4, 48, 768, 512], P(None, 'lat', 'lon')
- grad_qkv: bfloat16 [512, 1536], replicated
- grad_out: bfloat16 [512, 512], replicated
- grad_gain: float32 [512], replicated
All inputs are finite; a program needn't handle non-finite values.
Results may differ from a plain program's by a relative error of at most 0.014.
Values may be sent and summed in bfloat16 or wider, within the bound.
A program may use at most 64 MiB of HBM per device.

v0:
```python
import jax
import jax.numpy as jnp
from jax import lax
from jax.sharding import PartitionSpec as P

HEADS = 8
WIN_LEV = 2
WIN_LAT = 6
WIN_LON = 12


def passed_along(shard, axis, by):
    devices = lax.axis_size(axis)
    return lax.ppermute(shard, axis, [(i, (i + by) % devices) for i in range(devices)])


def to_windows(grid):
    lv, rows, cols, ch = grid.shape
    grid = grid.reshape(
        lv // WIN_LEV, WIN_LEV, rows // WIN_LAT, WIN_LAT, cols // WIN_LON, WIN_LON, ch
    )
    grid = grid.transpose(0, 2, 4, 1, 3, 5, 6)
    return grid.reshape(-1, WIN_LEV * WIN_LAT * WIN_LON, ch)


def from_windows(wins, lv, rows, cols):
    ch = wins.shape[-1]
    grid = wins.reshape(
        lv // WIN_LEV, rows // WIN_LAT, cols // WIN_LON, WIN_LEV, WIN_LAT, WIN_LON, ch
    )
    return grid.transpose(0, 3, 1, 4, 2, 5, 6).reshape(lv, rows, cols, ch)


def window_layer(x_win, g_win, labels, w_qkv, w_out, norm_gain_vector):
    nwin, span, ch = x_win.shape
    head_dim = ch // HEADS
    scale = head_dim ** (-0.5)
    f32 = jnp.float32
    same = labels[:, :, None] == labels[:, None, :]
    xf = x_win.astype(f32)
    centered_tokens = xf - jnp.mean(xf, axis=-1, keepdims=True)
    inverse_deviation = lax.rsqrt(
        jnp.mean(centered_tokens * centered_tokens, axis=-1, keepdims=True) + 1e-05
    )
    standardized_tokens = centered_tokens * inverse_deviation
    normalized_tokens = (standardized_tokens * norm_gain_vector).astype(jnp.bfloat16)
    qkv = jnp.einsum("wsc,cf->wsf", normalized_tokens, w_qkv, preferred_element_type=f32).astype(
        jnp.bfloat16
    )
    query = qkv[:, :, :ch].reshape(nwin, span, HEADS, head_dim)
    keys = qkv[:, :, ch : 2 * ch].reshape(nwin, span, HEADS, head_dim)
    values = qkv[:, :, 2 * ch :].reshape(nwin, span, HEADS, head_dim)
    scores = jnp.einsum("wshd,wthd->whst", query, keys, preferred_element_type=f32) * scale
    scores = jnp.where(same[:, None], scores, -jnp.inf)
    top = jnp.max(scores, axis=-1, keepdims=True)
    expo = jnp.exp(scores - top)
    probs = expo / jnp.sum(expo, axis=-1, keepdims=True)
    probs_b = probs.astype(jnp.bfloat16)
    attn = (
        jnp.einsum("whst,wthd->wshd", probs_b, values, preferred_element_type=f32)
        .astype(jnp.bfloat16)
        .reshape(nwin, span, ch)
    )
    branch = jnp.einsum("wsc,cd->wsd", attn, w_out, preferred_element_type=f32).astype(jnp.bfloat16)
    d_attn = jnp.einsum("wsd,cd->wsc", g_win, w_out, preferred_element_type=f32).astype(
        jnp.bfloat16
    )
    d_wout = jnp.einsum("wsc,wsd->cd", attn, g_win, preferred_element_type=f32)
    d_heads = d_attn.reshape(nwin, span, HEADS, head_dim)
    d_probs = jnp.einsum("wshd,wthd->whst", d_heads, values, preferred_element_type=f32)
    d_values = jnp.einsum("whst,wshd->wthd", probs_b, d_heads, preferred_element_type=f32).astype(
        jnp.bfloat16
    )
    d_scores = (
        probs * (d_probs - jnp.sum(d_probs * probs, axis=-1, keepdims=True)) * scale
    ).astype(jnp.bfloat16)
    d_query = jnp.einsum("whst,wthd->wshd", d_scores, keys, preferred_element_type=f32).astype(
        jnp.bfloat16
    )
    d_keys = jnp.einsum("whst,wshd->wthd", d_scores, query, preferred_element_type=f32).astype(
        jnp.bfloat16
    )
    d_qkv = jnp.concatenate(
        [
            d_query.reshape(nwin, span, ch),
            d_keys.reshape(nwin, span, ch),
            d_values.reshape(nwin, span, ch),
        ],
        axis=-1,
    )
    d_wqkv = jnp.einsum("wsc,wsf->cf", normalized_tokens, d_qkv, preferred_element_type=f32)
    normalized_gradient = jnp.einsum("wsf,cf->wsc", d_qkv, w_qkv, preferred_element_type=f32)
    gain_gradient = jnp.sum(normalized_gradient * standardized_tokens, axis=(0, 1))
    standardized_gradient = normalized_gradient * norm_gain_vector
    shifted_gradient = inverse_deviation * (
        standardized_gradient
        - jnp.mean(standardized_gradient, axis=-1, keepdims=True)
        - standardized_tokens
        * jnp.mean(standardized_gradient * standardized_tokens, axis=-1, keepdims=True)
    )
    return (branch, shifted_gradient.astype(jnp.bfloat16), d_wqkv, d_wout, gain_gradient)


def roll_in(stacked):
    half_lat = WIN_LAT // 2
    half_lon = WIN_LON // 2
    rows_below = passed_along(stacked[:, :, :half_lat], "lat", -1)
    shifted = jnp.concatenate([stacked[:, :, half_lat:], rows_below], axis=2)
    cols_east = passed_along(shifted[:, :, :, :half_lon], "lon", -1)
    shifted = jnp.concatenate([shifted[:, :, :, half_lon:], cols_east], axis=3)
    return jnp.roll(shifted, -(WIN_LEV // 2), axis=1)


def roll_out(grid):
    half_lat = WIN_LAT // 2
    half_lon = WIN_LON // 2
    grid = jnp.roll(grid, WIN_LEV // 2, axis=0)
    cols_west = passed_along(grid[:, :, -half_lon:], "lon", 1)
    grid = jnp.concatenate([cols_west, grid[:, :, :-half_lon]], axis=2)
    rows_above = passed_along(grid[:, -half_lat:], "lat", 1)
    return jnp.concatenate([rows_above, grid[:, :-half_lat]], axis=1)


def local(tokens, cotangent, w_qkv, w_out, norm_gain_vector):
    lv, rows, cols, ch = tokens.shape
    rolled_pair = roll_in(jnp.stack([tokens, cotangent]))
    band_rows = rows * lax.axis_size("lat")
    global_row = lax.axis_index("lat") * rows + jnp.arange(rows, dtype=jnp.int32)
    lat_label = (global_row >= band_rows - WIN_LAT // 2).astype(jnp.int32)
    lev_label = (jnp.arange(lv, dtype=jnp.int32) == lv - 1).astype(jnp.int32)
    label_grid = (
        2 * lat_label[None, :, None]
        + lev_label[:, None, None]
        + jnp.zeros((lv, rows, cols), jnp.int32)
    )
    labels = to_windows(label_grid[..., None])[..., 0]
    x_win = to_windows(rolled_pair[0])
    g_win = to_windows(rolled_pair[1])
    branch, shifted_gradient, d_wqkv, d_wout, gain_gradient = window_layer(
        x_win, g_win, labels, w_qkv, w_out, norm_gain_vector
    )
    branch_grid = roll_out(from_windows(branch, lv, rows, cols))
    layer_out = (tokens.astype(jnp.float32) + branch_grid.astype(jnp.float32)).astype(jnp.bfloat16)
    d_grid = roll_out(from_windows(shifted_gradient, lv, rows, cols))
    grad_tokens = (cotangent.astype(jnp.float32) + d_grid.astype(jnp.float32)).astype(jnp.bfloat16)
    total_qkv, total_out, total_gain = lax.psum((d_wqkv, d_wout, gain_gradient), ("lat", "lon"))
    return (
        layer_out,
        grad_tokens,
        total_qkv.astype(jnp.bfloat16),
        total_out.astype(jnp.bfloat16),
        total_gain,
    )


def solution(mesh):
    return jax.shard_map(
        local,
        mesh=mesh,
        in_specs=(P(None, "lat", "lon", None), P(None, "lat", "lon", None), P(), P(), P()),
        out_specs=(P(None, "lat", "lon", None), P(None, "lat", "lon", None), P(), P(), P()),
        check_vma=False,
    )
```

profile of v0, /device:TPU:1, one launch (start us, length us, event | category | flops | bytes accessed | tf_op | source)
XLA Modules:
  0.0 267.1 jit_solution(1011237223893658390)
XLA Ops:
  0.6 1.5 fusion.30
  2.1 6.1 %collective-permute-start = (bf16[2,4,3,24,512]{4,3,2,1,0:T(8,128)(2,1)S(1)}, bf16[2,4,3,24,512]{4,3,2,1,0:T(8,128)(2,1)S(1)}, u32[]{:S(2)}, u32[]{:S(2)}) collective-permute-start(bf16[2,4,3,24,512]{4,3,2,1,0:T(8,128)(2,1)S(1)} %get-tuple-element.27), channel_id=1, source_target_pairs={{0,224},{32,0},{64,32},{96,64},{128,96},{160,128},{192,160},{224,1... | collective-permute-start | bytes 1769480 | tf_op jit(solution)/shard_map/ppermute | solution.py:14
  8.5 11.7 %collective-permute-done = bf16[2,4,3,24,512]{4,3,2,1,0:T(8,128)(2,1)S(1)} collective-permute-done((bf16[2,4,3,24,512]{4,3,2,1,0:T(8,128)(2,1)S(1)}, bf16[2,4,3,24,512]{4,3,2,1,0:T(8,128)(2,1)S(1)}, u32[]{:S(2)}, u32[]{:S(2)}) %collective-permute-start) | collective-permute-done | bytes 589856 | tf_op jit(solution)/shard_map/ppermute | solution.py:14
  20.2 1.6 collective-permute-start.1
  23.0 5.9 %collective-permute-done.1 = bf16[2,4,6,6,512]{4,3,2,1,0:T(8,128)(2,1)S(1)} collective-permute-done((bf16[2,4,6,6,512]{4,3,2,1,0:T(8,128)(2,1)S(1)}, bf16[2,4,6,6,512]{4,3,2,1,0:T(8,128)(2,1)S(1)}, u32[]{:S(2)}, u32[]{:S(2)}) %collective-permute-start.1) | collective-permute-done | bytes 294944 | tf_op jit(solution)/shard_map/ppermute | solution.py:14
  29.1 1.4 fusion.46
  30.6 2.7 %reshape.171 = f32[2,2,1,6,2,12,512]{6,2,5,4,3,1,0:T(1,128)S(1)} reshape(f32[1,4,6,24,512]{4,3,2,1,0:T(8,128)} %get-tuple-element.25) | data formatting | bytes 2359296 | tf_op jit(solution)/shard_map/convert_element_type | solution.py:40
  34.4 2.4 multiply_reduce_fusion.3
  37.1 1.3 copy.102
  38.4 1.5 reshape.176
  42.2 2.2 copy.105
  44.4 2.2 copy.106
  47.9 1.5 copy.76
  52.6 1.7 convolution_convert_fusion.3
  55.6 4.6 %fusion.50 = f32[4,8,144,144]{2,3,1,0:T(8,128)} fusion(bf16[4,144,8,64]{1,3,2,0:T(8,128)(2,1)} %bitcast.81, bf16[4,144,8,64]{1,3,2,0:T(8,128)(2,1)} %bitcast.79), kind=kOutput, calls=%fused_computation.83 | convolution fusion | flops 84934656 | bytes 3833856 | tf_op jit(solution)/shard_map/wshd,wthd->whst/dot_general | solution.py:70
  60.2 5.5 %fusion.49 = (f32[4,8,144]{2,1,0:T(8,128)S(1)}, f32[4,8,144,144]{2,3,1,0:T(8,128)}) fusion(pred[4,144,144]{1,2,0:T(8,128)(4,1)S(1)} %copy-done.7, bf16[4,144,8,64]{1,3,2,0:T(8,128)(2,1)} %bitcast.88, bf16[4,144,8,64]{1,3,2,0:T(8,128)(2,1)} %bitcast.90), kind=kOutput, calls=%fused_computation.82 | convolution fusion | flops 87589008 | bytes 3935232 | tf_op jit(solution)/shard_map/sub | solution.py:56
  65.7 9.4 %fusion.20 = bf16[4,8,64,144]{3,2,1,0:T(8,128)(2,1)} fusion(bf16[4,144,8,64]{1,3,2,0:T(8,128)(2,1)} %bitcast.91, f32[4,8,144,144]{2,3,1,0:T(8,128)} %fusion.50, f32[4,8,144,144]{2,3,1,0:T(8,128)} %get-tuple-element.33, f32[4,8,144]{2,1,0:T(8,128)S(1)} %get-tuple-element.32), kind=kOutput, calls=%fused_computation.22 | convolution fusion | flops 89879184 | bytes 6506496 | tf_op jit(solution)/shard_map/whst,wthd->wshd/dot_general | solution.py:77
  75.2 9.4 %fusion.23 = bf16[4,8,64,144]{3,2,1,0:T(8,128)(2,1)} fusion(bf16[4,144,8,64]{1,3,2,0:T(8,128)(2,1)} %bitcast.89, f32[4,8,144,144]{2,3,1,0:T(8,128)} %fusion.50, f32[4,8,144,144]{2,3,1,0:T(8,128)} %get-tuple-element.33, f32[4,8,144]{2,1,0:T(8,128)S(1)} %get-tuple-element.32), kind=kOutput, calls=%fused_computation.23 | convolution fusion | flops 89879184 | bytes 6506496 | tf_op jit(solution)/shard_map/whst,wshd->wthd/dot_general | solution.py:80
  84.5 4.6 %convolution_convert_fusion.1 = bf16[4,8,64,144]{3,2,1,0:T(8,128)(2,1)} fusion(bf16[4,144,8,64]{1,3,2,0:T(8,128)(2,1)} %bitcast.82, f32[4,8,144,144]{2,3,1,0:T(8,128)} %get-tuple-element.33, f32[4,8,144]{2,1,0:T(8,128)S(1)} %get-tuple-element.32), kind=kOutput, calls=%fused_computation.24 | convolution fusion | flops 86556672 | bytes 3852288 | tf_op jit(solution)/shard_map/whst,wshd->wthd/dot_general | solution.py:71
  89.1 1.4 copy.87
  90.5 2.2 copy.88
  92.7 2.1 copy.89
  94.9 4.5 %convolution_bitcast_fusion = f32[512,1536]{1,0:T(8,128)} fusion(bf16[4,144,512]{2,1,0:T(8,128)(2,1)} %copy.89, bf16[4,144,512]{2,1,0:T(8,128)(2,1)} %copy.88, bf16[4,144,512]{2,1,0:T(8,128)(2,1)S(1)} %copy.87, f32[4,144,512]{2,1,0:T(8,128)S(1)} %reshape.176, f32[512]{0:T(512)S(1)} %copy-done.8, f32[4,144]{1,0:T(4,128)S(1)} %rsqrt.12, f32[4,144]{1,0:T(4,128)S(1)} %div.23), kind=kOutput, calls=%fused_computation.8 | convolution fusion | flops 912457728 | bytes 6101504 | tf_op jit(solution)/shard_map/wsc,wsf->cf/dot_general | solution.py:91
  99.4 1.6 multiply_reduce_fusion.1
  101.0 3.9 %convolution_convert_fusion.2 = bf16[4,8,64,144]{3,2,1,0:T(8,128)(2,1)} fusion(bf16[4,144,8,64]{1,3,2,0:T(8,128)(2,1)S(1)} %bitcast.80, f32[4,8,144,144]{2,3,1,0:T(8,128)} %get-tuple-element.33, f32[4,8,144]{2,1,0:T(8,128)S(1)} %get-tuple-element.32), kind=kOutput, calls=%fused_computation.25 | convolution fusion | flops 86556672 | bytes 3852288 | tf_op jit(solution)/shard_map/whst,wthd->wshd/dot_general | solution.py:60
  107.4 2.0 convolution_convert_fusion.4
  109.5 1.6 convolution_bitcast_fusion.1
  112.6 2.5 copy.74
  115.1 2.1 reshape.161
  117.7 1.9 collective-permute-start.2
  121.1 2.2 collective-permute-start.5
  125.6 138.5 %all-reduce.2 = (bf16[512,1536]{1,0:T(8,128)(2,1)}, bf16[512,512]{1,0:T(8,128)(2,1)}, f32[512]{0:T(512)}) all-reduce(f32[512,1536]{1,0:T(8,128)} %convolution_bitcast_fusion, f32[512,512]{1,0:T(8,128)} %convolution_bitcast_fusion.1, f32[512]{0:T(512)S(1)} %get-tuple-element.15), channel_id=1, replica_groups=mesh['lat'=8,'lon'=32] {'lat','lon'}, use_global_device_ids=true, to_apply=%region_7.8 | all-reduce | flops 1049088 | bytes 6295552 | tf_op jit(solution)/shard_map/psum | solution.py:146
  (70 shorter events, 22.4 us)
Async XLA Ops:
  0.6 39.3 %copy-start = (bf16[512,1536]{1,0:T(8,128)(2,1)S(1)}, bf16[512,1536]{1,0:T(8,128)(2,1)}, u32[]{:S(2)}) copy-start(bf16[512,1536]{1,0:T(8,128)(2,1)} %param.7) | copy-start | bytes 4718596
  2.1 18.1 %collective-permute-start = (bf16[2,4,3,24,512]{4,3,2,1,0:T(8,128)(2,1)S(1)}, bf16[2,4,3,24,512]{4,3,2,1,0:T(8,128)(2,1)S(1)}, u32[]{:S(2)}, u32[]{:S(2)}) collective-permute-start(bf16[2,4,3,24,512]{4,3,2,1,0:T(8,128)(2,1)S(1)} %get-tuple-element.27), channel_id=1, source_target_pairs={{0,224},{32,0},{64,32},{96,64},{128,96},{160,128},{192,160},{224,1... | collective-permute-start | bytes 1769480 | tf_op jit(solution)/shard_map/ppermute | solution.py:14
  20.2 8.6 %collective-permute-start.1 = (bf16[2,4,6,6,512]{4,3,2,1,0:T(8,128)(2,1)S(1)}, bf16[2,4,6,6,512]{4,3,2,1,0:T(8,128)(2,1)S(1)}, u32[]{:S(2)}, u32[]{:S(2)}) collective-permute-start(bf16[2,4,6,6,512]{4,3,2,1,0:T(8,128)(2,1)S(1)} %pad_maximum_fusion.7), channel_id=1, source_target_pairs={{0,31},{1,0},{2,1},{3,2},{4,3},{5,4},{6,5},{7,6},{8,7},{9,8},{10,9... | collective-permute-start | bytes 884744 | tf_op jit(solution)/shard_map/ppermute | solution.py:14
  38.4 1.5 copy-start.8
  55.6 4.6 %copy-start.7 = (pred[4,144,144]{1,2,0:T(8,128)(4,1)S(1)}, pred[4,144,144]{1,2,0:T(8,128)(4,1)}, u32[]{:S(2)}) copy-start(pred[4,144,144]{1,2,0:T(8,128)(4,1)} %broadcast_compare_fusion) | copy-start | bytes 248836
  94.9 4.6 %copy-start.5 = (bf16[4,144,512]{2,1,0:T(8,128)(2,1)S(1)}, bf16[4,144,512]{2,1,0:T(8,128)(2,1)}, u32[]{:S(2)}) copy-start(bf16[4,144,512]{2,1,0:T(8,128)(2,1)} %copy.88) | copy-start | bytes 1769476
  94.9 4.6 %copy-start.6 = (bf16[4,144,512]{2,1,0:T(8,128)(2,1)S(1)}, bf16[4,144,512]{2,1,0:T(8,128)(2,1)}, u32[]{:S(2)}) copy-start(bf16[4,144,512]{2,1,0:T(8,128)(2,1)} %copy.89) | copy-start | bytes 1769476
  99.4 1.6 copy-start.1
  107.1 2.3 copy-start.4
  107.2 2.3 copy-start.9
  107.3 12.3 %collective-permute-start.4 = (bf16[4,6,6,512]{3,0,2,1:T(4,128)(2,1)S(1)}, bf16[4,6,6,512]{3,0,2,1:T(4,128)(2,1)S(1)}, u32[]{:S(2)}, u32[]{:S(2)}) collective-permute-start(bf16[4,6,6,512]{3,0,2,1:T(4,128)(2,1)S(1)} %pad_maximum_fusion.8), channel_id=1, source_target_pairs={{0,1},{1,2},{2,3},{3,4},{4,5},{5,6},{6,7},{7,8},{8,9},{9,10},{10,1... | collective-permute-start | bytes 442376 | tf_op jit(solution)/shard_map/ppermute | solution.py:14
  117.7 5.6 %collective-permute-start.2 = (bf16[4,6,6,512]{3,0,2,1:T(4,128)(2,1)S(1)}, bf16[4,6,6,512]{3,0,2,1:T(4,128)(2,1)S(1)}, u32[]{:S(2)}, u32[]{:S(2)}) collective-permute-start(bf16[4,6,6,512]{3,0,2,1:T(4,128)(2,1)S(1)} %pad_maximum_fusion.9), channel_id=1, source_target_pairs={{0,1},{1,2},{2,3},{3,4},{4,5},{5,6},{6,7},{7,8},{8,9},{9,10},{10,1... | collective-permute-start | bytes 442376 | tf_op jit(solution)/shard_map/ppermute | solution.py:14
  121.1 143.0 %collective-permute-start.5 = (bf16[4,3,24,512]{3,0,2,1:T(4,128)(2,1)}, bf16[4,3,24,512]{3,0,2,1:T(4,128)(2,1)S(1)}, u32[]{:S(2)}, u32[]{:S(2)}) collective-permute-start(bf16[4,3,24,512]{3,0,2,1:T(4,128)(2,1)} %get-tuple-element.28), channel_id=1, source_target_pairs={{0,32},{32,64},{64,96},{96,128},{128,160},{160,192},{192,224},{224... | collective-permute-start | bytes 884744 | tf_op jit(solution)/shard_map/ppermute | solution.py:14
  124.7 140.9 %collective-permute-start.3 = (bf16[4,3,24,512]{3,0,2,1:T(4,128)(2,1)}, bf16[4,3,24,512]{3,0,2,1:T(4,128)(2,1)S(1)}, u32[]{:S(2)}, u32[]{:S(2)}) collective-permute-start(bf16[4,3,24,512]{3,0,2,1:T(4,128)(2,1)} %get-tuple-element.30), channel_id=1, source_target_pairs={{0,32},{32,64},{64,96},{96,128},{128,160},{160,192},{192,224},{224... | collective-permute-start | bytes 884744 | tf_op jit(solution)/shard_map/ppermute | solution.py:14
  125.6 138.5 %copy-start.2 = (bf16[4,6,24,512]{3,2,1,0:T(8,128)(2,1)S(1)}, bf16[4,6,24,512]{3,2,1,0:T(8,128)(2,1)}, u32[]{:S(2)}) copy-start(bf16[4,6,24,512]{3,2,1,0:T(8,128)(2,1)} %param.6) | copy-start | bytes 1769476
  264.1 1.5 copy-start.3
where the time goes:
time: 270 us; the launch traced here: 267 us
  blocking collectives  138 us (51%)
  matrix products  49.9 us (18%)
  local copies, waits for them, and re-layouts  36.4 us (13%)
  waiting for transfers between devices  17.6 us (7%)
  starting transfers between devices  12.8 us (5%)
  other arithmetic  10.9 us (4%)
    psum x1, blocking collectives, local(): lax.psum((d_wqkv, d_wout, gain_gradient), ('lat', 'lon'))  138 us
    ppermute x6, waiting for transfers between devices, passed_along(): lax.ppermute(shard, axis, [(i, (i + by) % devices) for i in range(devices)])  17.6 us
    ppermute x6, starting transfers between devices, passed_along(): lax.ppermute(shard, axis, [(i, (i + by) % devices) for i in range(devices)])  12.8 us
    dot_general x1, matrix products, window_layer(): jnp.einsum('whst,wthd->wshd', d_scores, keys, preferred_element_type=f32)  9.42 us
    dot_general x1, matrix products, window_layer(): jnp.einsum('whst,wshd->wthd', d_scores, query, preferred_element_type=f32)  9.37 us
    sub x1, matrix products, window_layer(): expo = jnp.exp(scores - top)  5.52 us
    convert_element_type x3, local copies, waits for them, and re-layouts, window_layer(): xf = x_win.astype(f32)  5.5 us
  transfers between devices with their start and end apart: 6, of which 2 were waited for; matrix products, arithmetic and copies ran while one was open for 6% of the time, Pallas kernels for 0%

commit v1 on v0

v1 whole, which is shorter than its diff:
```python
import functools

import jax
import jax.numpy as jnp
from jax import lax
from jax.experimental import pallas as pl
from jax.experimental.pallas import tpu as pltpu
from jax.sharding import PartitionSpec as P

CH = 512
HEADS = 8
HEAD_DIM = CH // HEADS
LEVELS = 4
ROWS = 6
HALF = 3
COLS = 24
SPAN = 144
CHUNK = 144
LAST_BAND = 7
GRADS = 4 * CH
SCALE = HEAD_DIM ** (-0.5)
LOG2E = 1.4426950408889634
MASKED = -1e30
LANES = 128
MESH = pl.DeviceIdType.MESH
f32 = jnp.float32
bf16 = jnp.bfloat16


def nt(a, b):
    return lax.dot_general(a, b, (((1,), (1,)), ((), ())), preferred_element_type=f32)


def tn(a, b):
    return lax.dot_general(a, b, (((0,), (0,)), ((), ())), preferred_element_type=f32)


def nn(a, b):
    return lax.dot_general(a, b, (((1,), (0,)), ((), ())), preferred_element_type=f32)


def turned(v, by):
    by = by % COLS
    return v if by == 0 else pltpu.roll(v, by, axis=0)


def place():
    lat, lon = lax.axis_index("lat"), lax.axis_index("lon")
    y, x_hi = lat // 2, lat % 2
    x_lo, z, core = lon // 16, (lon % 16) // 2, lon % 2
    return 2 * x_hi + x_lo, y, z, core


def device_at(x, y, z, core):
    return (2 * y + x // 2, 16 * (x % 2) + 2 * z + core)


def neighbour(by_lat, by_lon):
    lat, lon = lax.axis_index("lat"), lax.axis_index("lon")
    return ((lat + by_lat + 8) % 8, (lon + by_lon + 32) % 32)


def along(dim, k):
    x, y, z, core = place()
    if dim == "x":
        return device_at((x + k) % 4, y, z, core)
    if dim == "y":
        return device_at(x, (y + k) % 4, z, core)
    if dim == "z":
        return device_at(x, y, (z + k) % 8, core)
    return device_at(x, y, z, 1 - core)


def send(src, dst, sems, slot, device):
    return pltpu.make_async_remote_copy(
        src_ref=src,
        dst_ref=dst,
        send_sem=sems[0].at[slot],
        recv_sem=sems[1].at[slot],
        device_id=device,
        device_id_type=MESH,
    )


def greet(devices):
    barrier = pltpu.get_barrier_semaphore()
    for device in devices:
        pl.semaphore_signal(barrier, inc=1, device_id=device, device_id_type=MESH)
    pl.semaphore_wait(barrier, len(devices))


def pack_half(h, first, second, packed):
    row = lax.broadcasted_iota(jnp.int32, (COLS, LANES), 0)

    def lanes_step(c, _):
        lanes = pl.ds(pl.multiple_of(c * LANES, LANES), LANES)
        kinds = [[], [], [], []]
        for src in (first, second):
            for i in range(HALF):
                v0, v1, v2, v3 = (
                    src[l, HALF * h + i, :, lanes].astype(f32) for l in range(LEVELS)
                )
                kinds[0].append(jnp.where(row < 12, turned(v1, -6), turned(v2, 6)))
                kinds[1].append(jnp.where(row < 12, turned(v3, -6), turned(v0, 6)))
                kinds[2].append(
                    jnp.where(
                        row < 12,
                        jnp.where(row < 6, turned(v1, 6), turned(v2, 12)),
                        jnp.where(row < 18, turned(v3, 18), v0),
                    )
                )
                kinds[3].append(
                    jnp.where(
                        row < 12,
                        jnp.where(row < 6, v1, turned(v2, 6)),
                        jnp.where(row < 18, turned(v3, 12), turned(v0, 18)),
                    )
                )
        for kind in range(4):
            packed[h, kind, :, lanes] = jnp.concatenate(kinds[kind], axis=0).astype(bf16)
        return 0

    lax.fori_loop(0, CH // LANES, lanes_step, 0)


def unpack_half(h, chunks, first, second, first_out, second_out):
    row = lax.broadcasted_iota(jnp.int32, (COLS, LANES), 0)

    def lanes_step(c, _):
        lanes = pl.ds(pl.multiple_of(c * LANES, LANES), LANES)
        kinds = [chunks[kind][:, lanes].astype(f32) for kind in range(4)]
        for n, (src, out) in enumerate(((first, first_out), (second, second_out))):
            for i in range(HALF):
                at = 72 * n + COLS * i
                a0, a1, b, e = (kind[at : at + COLS] for kind in kinds)
                west, east = row < 6, row >= 18
                v1 = jnp.where(west, e, jnp.where(east, turned(b, 18), turned(a0, 6)))
                v2 = jnp.where(
                    west, turned(e, 18), jnp.where(east, turned(b, 12), turned(a0, 18))
                )
                v3 = jnp.where(
                    west, turned(e, 12), jnp.where(east, turned(b, 6), turned(a1, 6))
                )
                v0 = jnp.where(west, turned(e, 6), jnp.where(east, b, turned(a1, 18)))
                for l, v in enumerate((v0, v1, v2, v3)):
                    r = HALF * h + i
                    total = src[l, r, :, lanes].astype(f32) + v
                    out[l, r, :, lanes] = total.astype(bf16)
        return 0

    lax.fori_loop(0, CH // LANES, lanes_step, 0)


def by_pair(blocks):
    row = lax.broadcasted_iota(jnp.int32, blocks[0].shape, 0)
    pairs = ([], [])
    for j in range(3):
        a, b = blocks[2 * j], blocks[2 * j + 1]
        pairs[0].append(jnp.where(row < 12, a, turned(b, 12)))
        pairs[1].append(jnp.where(row < 12, turned(a, 12), b))
    return pairs


def by_row(pairs):
    row = lax.broadcasted_iota(jnp.int32, pairs[0][0].shape, 0)
    blocks = []
    for j in range(3):
        a, b = pairs[0][j], pairs[1][j]
        blocks.append(jnp.where(row < 12, a, turned(b, 12)))
        blocks.append(jnp.where(row < 12, turned(a, 12), b))
    return blocks


def blocks_of(value, n):
    return [value[72 * n + COLS * i : 72 * n + COLS * (i + 1)] for i in range(HALF)]


def set_bias(bias):
    last = (lax.axis_index("lat") == LAST_BAND).astype(jnp.int32)
    shape = (SPAN, SPAN)
    for s in range(2):
        labels = []
        for dim in range(2):
            i = lax.broadcasted_iota(jnp.int32, shape, dim)
            if s == 0:
                lat_row = i // COLS
                level = (i % COLS) // 12
            else:
                t = i % 72
                u = t % COLS
                lat_row = 2 * (t // COLS) + u // 12
                level = (u % 12) // 6
            labels.append((last * (lat_row < HALF).astype(jnp.int32), level))
        (kr, kl), (qr, ql) = labels
        same_row = kr == qr
        bias[s, 0] = jnp.where(same_row, 0.0, MASKED).astype(f32)
        bias[s, 1] = jnp.where(same_row & (kl == ql), 0.0, MASKED).astype(f32)


def norm_block(x, gain):
    mean = jnp.mean(x, axis=-1, keepdims=True)
    centered = x - mean
    inverse = lax.rsqrt(jnp.mean(centered * centered, axis=-1, keepdims=True) + 1e-05)
    xhat = centered * inverse
    return xhat, inverse, (xhat * gain).astype(bf16)


def load_windows(s, chunk_ref, gain_ref, normed, grads, xhat_ref, inverse_ref):
    gain = gain_ref[...]
    base = 2 * SPAN * s

    def store(off, xs, gs):
        x = jnp.concatenate(xs, axis=0)
        xhat, inverse, n = norm_block(x, gain)
        xhat_ref[off : off + 48] = xhat
        inverse_ref[off : off + 48] = jnp.broadcast_to(inverse, (48, LANES))
        normed[base + off : base + off + 48] = n
        grads[base + off : base + off + 48] = jnp.concatenate(gs, axis=0).astype(bf16)

    if s == 0:
        for p in range(2):
            halves = [chunk_ref(h, p)[...].astype(f32) for h in range(2)]
            xs = sum((blocks_of(v, 0) for v in halves), [])
            gs = sum((blocks_of(v, 1) for v in halves), [])
            for j in range(3):
                store(SPAN * p + 48 * j, xs[2 * j : 2 * j + 2], gs[2 * j : 2 * j + 2])
    else:
        parts = []
        for n in range(2):
            sides = []
            for kind in (2, 3):
                halves = [chunk_ref(h, kind)[...].astype(f32) for h in range(2)]
                sides.append(by_pair(sum((blocks_of(v, n) for v in halves), [])))
            parts.append([sides[0][p] + sides[1][p] for p in range(2)])
        for p in range(2):
            for j in range(3):
                store(
                    SPAN * p + 48 * j,
                    parts[0][p][2 * j : 2 * j + 2],
                    parts[1][p][2 * j : 2 * j + 2],
                )


def head_pair(s, p, lanes_of, bias, qkv, d_attn, attn, d_qkv):
    rows = slice(SPAN * p, SPAN * (p + 1))
    base = 2 * SPAN * s + SPAN * p
    out_rows = slice(base, base + SPAN)
    q = qkv[rows, lanes_of(0)]
    k = qkv[rows, lanes_of(1)]
    v = qkv[rows, lanes_of(2)]
    g = d_attn[rows, lanes_of(0)]
    lane = lax.broadcasted_iota(jnp.int32, (SPAN, LANES), 1)
    o, dq, dk, dv = [], [], [], []
    for e in range(2):
        mine = (lane < HEAD_DIM) if e == 0 else (lane >= HEAD_DIM)
        zero = jnp.zeros((), bf16)
        qm = jnp.where(mine, q, zero)
        km = jnp.where(mine, k, zero)
        vm = jnp.where(mine, v, zero)
        gm = jnp.where(mine, g, zero)
        scores = nt(k, qm) * (SCALE * LOG2E) + bias[s, p]
        top = jnp.max(scores, axis=0, keepdims=True)
        expo = jnp.exp2(scores - top)
        probs = expo * (1.0 / jnp.sum(expo, axis=0, keepdims=True))
        probs_b = probs.astype(bf16)
        d_probs = nt(v, gm)
        mean = jnp.sum(d_probs * probs, axis=0, keepdims=True)
        d_scores = (probs * (d_probs - mean) * SCALE).astype(bf16)
        o.append(tn(probs_b, vm))
        dv.append(nn(probs_b, gm))
        dq.append(tn(d_scores, km))
        dk.append(nn(d_scores, qm))
    attn[out_rows, lanes_of(0)] = (o[0] + o[1]).astype(bf16)
    d_qkv[out_rows, lanes_of(0)] = (dq[0] + dq[1]).astype(bf16)
    d_qkv[out_rows, lanes_of(1)] = (dk[0] + dk[1]).astype(bf16)
    d_qkv[out_rows, lanes_of(2)] = (dv[0] + dv[1]).astype(bf16)


def windows(s, chunk_ref, result_ref, w, scratch):
    w_qkv, w_out, gain_ref = w
    (normed, grads, attn, d_qkv, qkv, d_attn, xhat_ref, inverse_ref, branch, shifted, bias, gain_sum) = scratch
    base = 2 * SPAN * s
    rows = slice(base, base + 2 * SPAN)
    load_windows(s, chunk_ref, gain_ref, normed, grads, xhat_ref, inverse_ref)
    for n in range(3):
        cols = slice(CH * n, CH * (n + 1))
        qkv[:, cols] = nn(normed[rows], w_qkv[:, cols]).astype(bf16)
    d_attn[...] = nt(grads[rows], w_out[...]).astype(bf16)

    def pair_step(hp, _):
        def lanes_of(n):
            return pl.ds(pl.multiple_of(CH * n + LANES * hp, LANES), LANES)

        for p in range(2):
            head_pair(s, p, lanes_of, bias, qkv, d_attn, attn, d_qkv)
        return 0

    lax.fori_loop(0, HEADS // 2, pair_step, 0)
    branch[...] = nn(attn[rows], w_out[...])
    shifted[...] = nt(d_qkv[rows], w_qkv[...])
    gain = gain_ref[...]
    for i in range(6):
        at = slice(48 * i, 48 * (i + 1))
        d_normed = shifted[at]
        xhat = xhat_ref[at]
        gain_sum[...] += jnp.sum((d_normed * xhat).reshape(6, 8, CH), axis=0)
        d_xhat = d_normed * gain
        mean = jnp.mean(d_xhat, axis=-1, keepdims=True)
        slope = jnp.mean(d_xhat * xhat, axis=-1, keepdims=True)
        shifted[at] = inverse_ref[at, 0:1] * (d_xhat - mean - xhat * slope)
    if s == 0:
        for p in range(2):
            for h in range(2):
                at = slice(SPAN * p + 72 * h, SPAN * p + 72 * (h + 1))
                result_ref(h, p)[...] = jnp.concatenate(
                    [branch[at], shifted[at]], axis=0
                ).astype(bf16)
    else:
        for side, kind in enumerate((2, 3)):
            blocks = []
            for value in (branch, shifted):
                pairs = [
                    [
                        value[SPAN * p + 72 * side + COLS * j : SPAN * p + 72 * side + COLS * (j + 1)]
                        for j in range(3)
                    ]
                    for p in range(2)
                ]
                blocks.append(by_row(pairs))
            for h in range(2):
                result_ref(h, kind)[...] = jnp.concatenate(
                    blocks[0][HALF * h : HALF * h + HALF] + blocks[1][HALF * h : HALF * h + HALF],
                    axis=0,
                ).astype(bf16)


def weight_grads(n, total, scratch):
    normed, grads, attn, d_qkv = scratch[:4]
    cols = slice(CH * n, CH * (n + 1))
    if n < 3:
        total[:, cols] = tn(normed[...], d_qkv[:, cols]).astype(bf16)
    else:
        total[:, cols] = tn(attn[...], grads[...]).astype(bf16)


def gain_rows(gain_sum, gain_out):
    row = jnp.sum(gain_sum[...], axis=0, keepdims=True)
    gain_out[...] = jnp.concatenate(
        [row[:, LANES * i : LANES * (i + 1)] for i in range(4)] + [jnp.zeros((4, LANES), f32)],
        axis=0,
    )


WINDOW_SCRATCH = [
    pltpu.VMEM((4 * SPAN, CH), bf16),
    pltpu.VMEM((4 * SPAN, CH), bf16),
    pltpu.VMEM((4 * SPAN, CH), bf16),
    pltpu.VMEM((4 * SPAN, 3 * CH), bf16),
    pltpu.VMEM((2 * SPAN, 3 * CH), bf16),
    pltpu.VMEM((2 * SPAN, CH), bf16),
    pltpu.VMEM((2 * SPAN, CH), f32),
    pltpu.VMEM((2 * SPAN, LANES), f32),
    pltpu.VMEM((2 * SPAN, CH), f32),
    pltpu.VMEM((2 * SPAN, CH), f32),
    pltpu.VMEM((2, 2, SPAN, SPAN), f32),
    pltpu.VMEM((8, CH), f32),
]


def compute_kernel(work, w_qkv, w_out, gain, result, total, gain_out, *scratch):
    set_bias(scratch[10])
    scratch[11][...] = jnp.zeros((8, CH), f32)
    for s in range(2):
        windows(
            s,
            lambda h, kind: work.at[h, kind],
            lambda h, kind: result.at[h, kind],
            (w_qkv, w_out, gain),
            scratch,
        )
    gain_rows(scratch[11], gain_out)
    for n in range(4):
        weight_grads(n, total, scratch)


FLOWS = (("x", "y"), ("y", "x"))
FLOW_COLS = GRADS // 2


def partners():
    return (
        [along("core", 0)]
        + [along("x", k) for k in (1, 2, 3)]
        + [along("y", k) for k in (1, 2, 3)]
        + [along("z", k) for k in range(1, 8)]
    )


SUM_SCRATCH = [
    pltpu.VMEM((256, GRADS), bf16),
    pltpu.VMEM((256, GRADS), bf16),
    pltpu.VMEM((2, 3, 64, FLOW_COLS), bf16),
    pltpu.VMEM((2, 64, FLOW_COLS), bf16),
    pltpu.VMEM((2, 3, 16, FLOW_COLS), bf16),
    pltpu.VMEM((2, 16, FLOW_COLS), bf16),
    pltpu.VMEM((2, 7, 16, LANES), bf16),
    pltpu.VMEM((14, 8, LANES), f32),
    pltpu.VMEM((4, 8, LANES), f32),
    pltpu.SemaphoreType.DMA((2, 4)),
    pltpu.SemaphoreType.DMA((2, 6)),
    pltpu.SemaphoreType.DMA((2, 6)),
    pltpu.SemaphoreType.DMA((2, 14)),
    pltpu.SemaphoreType.DMA((2, 14)),
    pltpu.SemaphoreType.DMA((2, 14)),
    pltpu.SemaphoreType.DMA((2, 6)),
    pltpu.SemaphoreType.DMA((2, 6)),
    pltpu.SemaphoreType.DMA((2, 8)),
]


def multiple(value, of):
    return pl.multiple_of(value, of)


class Sums:
    def __init__(self, total, out, gain_in, gain_out, scratch):
        self.total, self.out, self.gain_in, self.gain_out = total, out, gain_in, gain_out
        (self.r0, self.b1, self.r1, self.b2, self.r2, self.b3, self.r3, self.gr, self.gs) = scratch[:9]
        sems = [(s.at[0], s.at[1]) for s in scratch[9:]]
        (self.s0, self.s1, self.s2, self.s3, self.sg, self.t3, self.t2, self.t1, self.t0) = sems
        self.x, self.y, self.z, self.core = place()
        self.at = {"x": self.x, "y": self.y, "z": self.z}
        self.started = []

    def go(self, copy):
        copy.start()
        self.started.append(copy)
        return copy

    def core_send(self, n):
        cols = slice(CH * n, CH * (n + 1))
        theirs = pl.ds(multiple((1 - self.core) * 256, 256), 256)
        return self.go(
            send(self.total.at[theirs, cols], self.r0.at[:, cols], self.s0, n, along("core", 0))
        )

    def core_add(self, n):
        cols = slice(CH * n, CH * (n + 1))

        def step(i, _):
            here = pl.ds(multiple(i * 64, 64), 64)
            mine = pl.ds(multiple(self.core * 256 + i * 64, 64), 64)
            self.b1[here, cols] = (
                self.total[mine, cols].astype(f32) + self.r0[here, cols].astype(f32)
            ).astype(bf16)
            return 0

        lax.fori_loop(0, 4, step, 0)

    def first_send(self, f):
        d = FLOWS[f][0]
        cols = slice(FLOW_COLS * f, FLOW_COLS * (f + 1))
        copies = []
        for k in (1, 2, 3):
            theirs = pl.ds(multiple((self.at[d] + k) % 4 * 64, 64), 64)
            copies.append(
                self.go(send(self.b1.at[theirs, cols], self.r1.at[f, k - 1], self.s1, 3 * f + k - 1, along(d, k)))
            )
        return copies

    def first_add(self, f):
        d = FLOWS[f][0]
        cols = slice(FLOW_COLS * f, FLOW_COLS * (f + 1))

        def step(i, _):
            here = pl.ds(multiple(i * 16, 16), 16)
            mine = pl.ds(multiple(self.at[d] * 64 + i * 16, 16), 16)
            total = self.b1[mine, cols].astype(f32)
            for k in range(3):
                total += self.r1[f, k, here].astype(f32)
            self.b2[f, here] = total.astype(bf16)
            return 0

        lax.fori_loop(0, 4, step, 0)

    def second_send(self, f):
        d = FLOWS[f][1]
        copies = []
        for k in (1, 2, 3):
            theirs = pl.ds(multiple((self.at[d] + k) % 4 * 16, 16), 16)
            copies.append(
                self.go(send(self.b2.at[f, theirs], self.r2.at[f, k - 1], self.s2, 3 * f + k - 1, along(d, k)))
            )
        return copies

    def second_add(self, f):
        d = FLOWS[f][1]
        mine = pl.ds(multiple(self.at[d] * 16, 16), 16)
        total = self.b2[f, mine].astype(f32)
        for k in range(3):
            total += self.r2[f, k].astype(f32)
        self.b3[f] = total.astype(bf16)

    def third_send(self, f):
        copies = []
        for k in range(1, 8):
            theirs = pl.ds(multiple((self.z + k) % 8 * LANES, LANES), LANES)
            copies.append(
                self.go(send(self.b3.at[f, :, theirs], self.r3.at[f, k - 1], self.s3, 7 * f + k - 1, along("z", k)))
            )
        return copies

    def rows(self, f, depth):
        start = self.core * 256
        if depth >= 1:
            start = start + self.at[FLOWS[f][0]] * 64
        if depth >= 2:
            start = start + self.at[FLOWS[f][1]] * 16
        size = (256, 64, 16)[depth]
        return pl.ds(multiple(start, size), size)

    def cols(self, f):
        return pl.ds(multiple(FLOW_COLS * f + self.z * LANES, LANES), LANES)

    def third_add(self, f):
        mine = pl.ds(multiple(self.z * LANES, LANES), LANES)
        total = self.b3[f, :, mine].astype(f32)
        for k in range(7):
            total += self.r3[f, k].astype(f32)
        self.out[self.rows(f, 2), self.cols(f)] = total.astype(bf16)

    def spread_third(self, f):
        here = self.out.at[self.rows(f, 2), self.cols(f)]
        return [self.go(send(here, here, self.t3, 7 * f + k - 1, along("z", k))) for k in range(1, 8)]

    def spread_second(self, f):
        here = self.out.at[self.rows(f, 2), FLOW_COLS * f : FLOW_COLS * (f + 1)]
        return [self.go(send(here, here, self.t2, 3 * f + k - 1, along(FLOWS[f][1], k))) for k in (1, 2, 3)]

    def spread_first(self, f):
        here = self.out.at[self.rows(f, 1), FLOW_COLS * f : FLOW_COLS * (f + 1)]
        return [self.go(send(here, here, self.t1, 3 * f + k - 1, along(FLOWS[f][0], k))) for k in (1, 2, 3)]

    def spread_core(self, f, k):
        start = self.core * 256 + (self.at[FLOWS[f][0]] + 4 - k) % 4 * 64
        here = self.out.at[pl.ds(multiple(start, 64), 64), FLOW_COLS * f : FLOW_COLS * (f + 1)]
        return self.go(send(here, here, self.t0, 4 * f + k, along("core", 0)))

    def gain_send(self, stage):
        dim, slots = (("core", (0,)), ("x", (1, 2, 3)), ("y", (4, 5, 6)), ("z", tuple(range(7, 14))))[stage]
        src = self.gain_in if stage == 0 else self.gs.at[stage - 1]
        return [
            self.go(send(src, self.gr.at[slot], self.sg, slot, along(dim, i + 1)))
            for i, slot in enumerate(slots)
        ]

    def gain_add(self, stage, copies):
        slots = ((0,), (1, 2, 3), (4, 5, 6), tuple(range(7, 14)))[stage]
        total = self.gain_in[...] if stage == 0 else self.gs[stage - 1]
        for slot, copy in zip(slots, copies):
            copy.wait_recv()
            total = total + self.gr[slot]
        if stage == 3:
            self.gain_out[...] = total
        else:
            self.gs[stage] = total

    def after_core(self, core_copies, gain_copies):
        first, second, third, spread = {}, {}, {}, {}
        for f in range(2):
            for n in (2 * f, 2 * f + 1):
                core_copies[n].wait_recv()
                self.core_add(n)
            first[f] = self.first_send(f)
        self.gain_add(0, gain_copies)
        gain_copies = self.gain_send(1)
        for f in range(2):
            for copy in first[f]:
                copy.wait_recv()
            self.first_add(f)
            second[f] = self.second_send(f)
        self.gain_add(1, gain_copies)
        gain_copies = self.gain_send(2)
        for f in range(2):
            for copy in second[f]:
                copy.wait_recv()
            self.second_add(f)
            third[f] = self.third_send(f)
        self.gain_add(2, gain_copies)
        gain_copies = self.gain_send(3)
        for f in range(2):
            for copy in third[f]:
                copy.wait_recv()
            self.third_add(f)
            spread[f] = self.spread_third(f)
        self.gain_add(3, gain_copies)
        for f in range(2):
            for copy in spread[f]:
                copy.wait_recv()
            spread[f] = self.spread_second(f)
        for f in range(2):
            for copy in spread[f]:
                copy.wait_recv()
            spread[f] = self.spread_first(f)
        last = []
        for f in range(2):
            last.append(self.spread_core(f, 0))
        for k in range(3):
            for f in range(2):
                spread[f][k].wait_recv()
                last.append(self.spread_core(f, k + 1))
        return last

    def finish(self, last):
        for copy in last:
            copy.wait_recv()
        for copy in self.started:
            copy.wait_send()


ROUTES = ((0, 0, 1, 0), (0, 1, 1, 0), (0, 2, 1, 0), (0, 3, 1, 1), (1, 3, 0, 1))


def halo_neighbours():
    return [neighbour(s * a, s * b) for s in (1, -1) for a, b in ((1, 0), (0, 1), (1, 1))]


def in_kernel(tokens, cotangent, work, packed, sems):
    greet(halo_neighbours())
    copies = []
    for h in range(2):
        pack_half(h, tokens, cotangent, packed)
        for n, (hh, kind, a, b) in enumerate(ROUTES):
            if hh == h:
                copies.append(
                    send(packed.at[h, kind], work.at[h, kind], (sems.at[0], sems.at[1]), n, neighbour(-a, -b))
                )
                copies[-1].start()
    for kind in range(3):
        work[1, kind] = packed[1, kind]
    for copy in copies:
        copy.wait()


def out_kernel(
    result, total, gain_in, tokens, cotangent, layer_out, grad_tokens, out, gain_out, back, sems, *scratch
):
    greet(halo_neighbours() + partners())
    sums = Sums(total, out, gain_in, gain_out, scratch)
    core_copies = [sums.core_send(n) for n in range(4)]
    gain_copies = sums.gain_send(0)
    copies = []
    for n, (h, kind, a, b) in enumerate(ROUTES):
        copies.append(
            send(result.at[h, kind], back.at[n], (sems.at[0], sems.at[1]), n, neighbour(a, b))
        )
        copies[-1].start()
    last = sums.after_core(core_copies, gain_copies)
    for copy in copies:
        copy.wait_recv()
    unpack_half(0, [back.at[n] for n in range(4)], tokens, cotangent, layer_out, grad_tokens)
    unpack_half(
        1,
        [result.at[1, kind] for kind in range(3)] + [back.at[4]],
        tokens,
        cotangent,
        layer_out,
        grad_tokens,
    )
    sums.finish(last)
    for copy in copies:
        copy.wait_send()


VMEM = pl.BlockSpec(memory_space=pltpu.VMEM)
LIMIT = 56 * 1024 * 1024


def local(tokens, cotangent, w_qkv, w_out, norm_gain_vector):
    gain = norm_gain_vector.reshape(1, CH)
    shape = jax.ShapeDtypeStruct
    work = pl.pallas_call(
        in_kernel,
        out_shape=shape((2, 4, CHUNK, CH), bf16),
        in_specs=[VMEM] * 2,
        out_specs=VMEM,
        scratch_shapes=[pltpu.VMEM((2, 4, CHUNK, CH), bf16), pltpu.SemaphoreType.DMA((2, 5))],
        compiler_params=pltpu.CompilerParams(
            collective_id=0, has_side_effects=True, vmem_limit_bytes=LIMIT
        ),
    )(tokens, cotangent)
    result, total, gain_in = pl.pallas_call(
        compute_kernel,
        out_shape=(
            shape((2, 4, CHUNK, CH), bf16),
            shape((CH, GRADS), bf16),
            shape((8, LANES), f32),
        ),
        in_specs=[VMEM] * 4,
        out_specs=(VMEM,) * 3,
        scratch_shapes=WINDOW_SCRATCH,
        compiler_params=pltpu.CompilerParams(vmem_limit_bytes=LIMIT),
    )(work, w_qkv, w_out, gain)
    layer_out, grad_tokens, out, gain_out = pl.pallas_call(
        out_kernel,
        out_shape=(
            shape(tokens.shape, bf16),
            shape(tokens.shape, bf16),
            shape((CH, GRADS), bf16),
            shape((8, LANES), f32),
        ),
        in_specs=[VMEM] * 5,
        out_specs=(VMEM,) * 4,
        scratch_shapes=[pltpu.VMEM((5, CHUNK, CH), bf16), pltpu.SemaphoreType.DMA((2, 5))]
        + SUM_SCRATCH,
        compiler_params=pltpu.CompilerParams(
            collective_id=1, has_side_effects=True, vmem_limit_bytes=LIMIT
        ),
    )(result, total, gain_in, tokens, cotangent)
    return (
        layer_out,
        grad_tokens,
        out[:, : 3 * CH],
        out[:, 3 * CH :],
        gain_out[:4].reshape(CH),
    )


def solution(mesh):
    return jax.shard_map(
        local,
        mesh=mesh,
        in_specs=(P(None, "lat", "lon", None), P(None, "lat", "lon", None), P(), P(), P()),
        out_specs=(P(None, "lat", "lon", None), P(None, "lat", "lon", None), P(), P(), P()),
        check_vma=False,
    )
```

time: 270 us -> 112 us (0.41); the launches traced: 267 us -> 112 us
  blocking collectives: 138 us -> 0 us
  Pallas kernels: 0 us -> 104 us
  matrix products: 49.9 us -> 0 us
  local copies, waits for them, and re-layouts: 36.4 us -> 7.51 us
  waiting for transfers between devices: 17.6 us -> 0 us
  starting transfers between devices: 12.8 us -> 0 us
  other arithmetic: 10.9 us -> 0 us
    psum x1 -> x0, blocking collectives: 138 us -> none  [local(): lax.psum((d_wqkv, d_wout, gain_gradient), ('lat', 'lon'))]
    pallas_call x0 -> x3, Pallas kernels: none -> 104 us  [the longest x1 65.2 us: local(): pl.pallas_call(out_kernel, out_shape=(shape(tokens.shape, bf16), shape(to...]
    dot_general x11 -> x0, matrix products: 44.4 us -> none  [the longest x1 9.42 us: window_layer(): jnp.einsum('whst,wthd->wshd', d_scores, keys, preferred_element_type=f32)]
    ppermute x6 -> x0, waiting for transfers between devices: 17.6 us -> none  [passed_along(): lax.ppermute(shard, axis, [(i, (i + by) % devices) for i in range(devices)])]
    reshape x13 -> x1, local copies, waits for them, and re-layouts: 18.4 us -> 1.26 us  [local(): gain_out[:4].reshape(CH)]
    ppermute x6 -> x0, starting transfers between devices: 12.8 us -> none  [passed_along(): lax.ppermute(shard, axis, [(i, (i + by) % devices) for i in range(devices)])]
    convert_element_type x5 -> x0, local copies, waits for them, and re-layouts: 6.41 us -> none  [the longest x3 5.5 us: window_layer(): xf = x_win.astype(f32)]
    sub x1 -> x0, matrix products: 5.52 us -> none  [window_layer(): expo = jnp.exp(scores - top)]
  transfers between devices with their start and end apart: 6 -> 0, of which waited for: 2 -> 0; matrix products, arithmetic and copies ran while one was open for 6% -> 0% of each run, Pallas kernels for 0% -> 0%
where the time goes in v1:
time: 112 us
  Pallas kernels  104 us (93%)
  local copies, waits for them, and re-layouts  7.51 us (7%)
    pallas_call x1, Pallas kernels, local(): pl.pallas_call(out_kernel, out_shape=(shape(tokens.shape, bf16), shape(to...  65.2 us
    pallas_call x1, Pallas kernels, local(): pl.pallas_call(in_kernel, out_shape=shape((2, 4, CHUNK, CH), bf16), in_sp...  20.6 us
    pallas_call x1, Pallas kernels, local(): pl.pallas_call(compute_kernel, out_shape=(shape((2, 4, CHUNK, CH), bf16),...  17.9 us
    slice x1, local copies, waits for them, and re-layouts, local(): out[:, :3 * CH]  2.75 us

profile of v1, /device:TPU:1, one launch (start us, length us, event | category | flops | bytes accessed | tf_op | source)
XLA Modules:
  0.0 111.8 jit_solution(13229043679187981338)
XLA Ops:
  0.6 20.6 %shard_map.92.work = bf16[2,4,144,512]{3,2,1,0:T(8,128)(2,1)} custom-call(bf16[4,6,24,512]{3,2,1,0:T(8,128)(2,1)} %tokens.3, bf16[4,6,24,512]{3,2,1,0:T(8,128)(2,1)} %cotangent.3), custom_call_target="tpu_custom_call" | custom-call | tf_op jit(solution)/shard_map/pallas_call | solution.py:682
  21.3 17.9 %shard_map.93 = (bf16[2,4,144,512]{3,2,1,0:T(8,128)(2,1)}, bf16[512,2048]{1,0:T(8,128)(2,1)}, f32[8,128]{1,0:T(8,128)}) custom-call(bf16[2,4,144,512]{3,2,1,0:T(8,128)(2,1)} %shard_map.92.work, bf16[512,1536]{1,0:T(8,128)(2,1)} %w_qkv.1, bf16[512,512]{1,0:T(8,128)(2,1)} %w_out.1, f32[1,512]{1,0:T(1,128)} %bitcast.3), custom_call_target="tpu_custom_call" | custom-call | tf_op jit(solution)/shard_map/pallas_call | solution.py:692
  39.1 65.2 %shard_map.94 = (bf16[4,6,24,512]{3,2,1,0:T(8,128)(2,1)}, bf16[4,6,24,512]{3,2,1,0:T(8,128)(2,1)}, bf16[512,2048]{1,0:T(8,128)(2,1)}, f32[8,128]{1,0:T(8,128)}) custom-call(bf16[2,4,144,512]{3,2,1,0:T(8,128)(2,1)} %get-tuple-element.12.result, bf16[512,2048]{1,0:T(8,128)(2,1)} %get-tuple-element.13.total, f32[8,128]{1,0:T(8,128)} %get-tuple-element.14.gain_in, ...), custom_call_target="tpu_custom_call" | custom-call | tf_op jit(solution)/shard_map/pallas_call | solution.py:704
  104.3 1.3 %slice_bitcast_fusion = f32[512]{0:T(512)} fusion(f32[8,128]{1,0:T(8,128)} %get-tuple-element.18), kind=kLoop, calls=%fused_computation | loop fusion | bytes 4096 | tf_op jit(solution)/shard_map/reshape | solution.py:725
  105.5 1.9 %slice.10 = bf16[512,512]{1,0:T(8,128)(2,1)} slice(bf16[512,2048]{1,0:T(8,128)(2,1)} %get-tuple-element.17), slice={[0:512], [1536:2048]} | slice | bytes 1048576 | tf_op jit(solution)/shard_map/slice | solution.py:724
  107.4 0.0 copy-start.1
  107.4 0.0 copy-start
  107.4 2.7 %slice.9 = bf16[512,1536]{1,0:T(8,128)(2,1)} slice(bf16[512,2048]{1,0:T(8,128)(2,1)} %get-tuple-element.17), slice={[0:512], [0:1536]} | slice | bytes 3145728 | tf_op jit(solution)/shard_map/slice | solution.py:723
  110.2 0.0 copy-done.1
  110.2 0.8 copy.12
  111.0 0.0 copy-done
  111.0 0.8 copy.13
Async XLA Ops:
  107.4 2.8 %copy-start.1 = (bf16[4,6,24,512]{3,2,1,0:T(8,128)(2,1)S(1)}, bf16[4,6,24,512]{3,2,1,0:T(8,128)(2,1)}, u32[]{:S(2)}) copy-start(bf16[4,6,24,512]{3,2,1,0:T(8,128)(2,1)} %get-tuple-element.24) | copy-start | bytes 1769476
  107.4 3.6 %copy-start = (bf16[4,6,24,512]{3,2,1,0:T(8,128)(2,1)S(1)}, bf16[4,6,24,512]{3,2,1,0:T(8,128)(2,1)}, u32[]{:S(2)}) copy-start(bf16[4,6,24,512]{3,2,1,0:T(8,128)(2,1)} %get-tuple-element.25) | copy-start | bytes 1769476

commit v2 on v1

v2 whole, which is shorter than its diff:
```python
import functools

import jax
import jax.numpy as jnp
from jax import lax
from jax.experimental import pallas as pl
from jax.experimental.pallas import tpu as pltpu
from jax.sharding import PartitionSpec as P

CH = 512
HEADS = 8
HEAD_DIM = CH // HEADS
LEVELS = 4
ROWS = 6
HALF = 3
COLS = 24
SPAN = 144
CHUNK = 144
LAST_BAND = 7
GRADS = 4 * CH
SCALE = HEAD_DIM ** (-0.5)
LOG2E = 1.4426950408889634
MASKED = -1e30
LANES = 128
MESH = pl.DeviceIdType.MESH
f32 = jnp.float32
bf16 = jnp.bfloat16


def nt(a, b):
    return lax.dot_general(a, b, (((1,), (1,)), ((), ())), preferred_element_type=f32)


def tn(a, b):
    return lax.dot_general(a, b, (((0,), (0,)), ((), ())), preferred_element_type=f32)


def nn(a, b):
    return lax.dot_general(a, b, (((1,), (0,)), ((), ())), preferred_element_type=f32)


def turned(v, by):
    by = by % COLS
    return v if by == 0 else pltpu.roll(v, by, axis=0)


def place():
    lat, lon = lax.axis_index("lat"), lax.axis_index("lon")
    y, x_hi = lat // 2, lat % 2
    x_lo, z, core = lon // 16, (lon % 16) // 2, lon % 2
    return 2 * x_hi + x_lo, y, z, core


def device_at(x, y, z, core):
    return (2 * y + x // 2, 16 * (x % 2) + 2 * z + core)


def neighbour(by_lat, by_lon):
    lat, lon = lax.axis_index("lat"), lax.axis_index("lon")
    return ((lat + by_lat + 8) % 8, (lon + by_lon + 32) % 32)


def along(dim, k):
    x, y, z, core = place()
    if dim == "x":
        return device_at((x + k) % 4, y, z, core)
    if dim == "y":
        return device_at(x, (y + k) % 4, z, core)
    if dim == "z":
        return device_at(x, y, (z + k) % 8, core)
    return device_at(x, y, z, 1 - core)


def send(src, dst, sems, slot, device):
    return pltpu.make_async_remote_copy(
        src_ref=src,
        dst_ref=dst,
        send_sem=sems[0].at[slot],
        recv_sem=sems[1].at[slot],
        device_id=device,
        device_id_type=MESH,
    )


def greet(devices):
    for device in devices:
        pl.semaphore_signal(
            pltpu.get_barrier_semaphore(), inc=1, device_id=device, device_id_type=MESH
        )


def pack_half(h, first, second, packed):
    row = lax.broadcasted_iota(jnp.int32, (COLS, LANES), 0)

    def lanes_step(c, _):
        lanes = pl.ds(pl.multiple_of(c * LANES, LANES), LANES)
        kinds = [[], [], [], []]
        for src in (first, second):
            for i in range(HALF):
                v0, v1, v2, v3 = (
                    src[l, HALF * h + i, :, lanes].astype(f32) for l in range(LEVELS)
                )
                kinds[0].append(jnp.where(row < 12, turned(v1, -6), turned(v2, 6)))
                kinds[1].append(jnp.where(row < 12, turned(v3, -6), turned(v0, 6)))
                kinds[2].append(
                    jnp.where(
                        row < 12,
                        jnp.where(row < 6, turned(v1, 6), turned(v2, 12)),
                        jnp.where(row < 18, turned(v3, 18), v0),
                    )
                )
                kinds[3].append(
                    jnp.where(
                        row < 12,
                        jnp.where(row < 6, v1, turned(v2, 6)),
                        jnp.where(row < 18, turned(v3, 12), turned(v0, 18)),
                    )
                )
        for kind in range(4):
            packed[h, kind, :, lanes] = jnp.concatenate(kinds[kind], axis=0).astype(bf16)
        return 0

    lax.fori_loop(0, CH // LANES, lanes_step, 0)


def unpack_half(h, chunks, first, second, first_out, second_out):
    row = lax.broadcasted_iota(jnp.int32, (COLS, LANES), 0)

    def lanes_step(c, _):
        lanes = pl.ds(pl.multiple_of(c * LANES, LANES), LANES)
        kinds = [chunks[kind][:, lanes].astype(f32) for kind in range(4)]
        for n, (src, out) in enumerate(((first, first_out), (second, second_out))):
            for i in range(HALF):
                at = 72 * n + COLS * i
                a0, a1, b, e = (kind[at : at + COLS] for kind in kinds)
                west, east = row < 6, row >= 18
                v1 = jnp.where(west, e, jnp.where(east, turned(b, 18), turned(a0, 6)))
                v2 = jnp.where(
                    west, turned(e, 18), jnp.where(east, turned(b, 12), turned(a0, 18))
                )
                v3 = jnp.where(
                    west, turned(e, 12), jnp.where(east, turned(b, 6), turned(a1, 6))
                )
                v0 = jnp.where(west, turned(e, 6), jnp.where(east, b, turned(a1, 18)))
                for l, v in enumerate((v0, v1, v2, v3)):
                    r = HALF * h + i
                    total = src[l, r, :, lanes].astype(f32) + v
                    out[l, r, :, lanes] = total.astype(bf16)
        return 0

    lax.fori_loop(0, CH // LANES, lanes_step, 0)


def by_pair(blocks):
    row = lax.broadcasted_iota(jnp.int32, blocks[0].shape, 0)
    pairs = ([], [])
    for j in range(3):
        a, b = blocks[2 * j], blocks[2 * j + 1]
        pairs[0].append(jnp.where(row < 12, a, turned(b, 12)))
        pairs[1].append(jnp.where(row < 12, turned(a, 12), b))
    return pairs


def by_row(pairs):
    row = lax.broadcasted_iota(jnp.int32, pairs[0][0].shape, 0)
    blocks = []
    for j in range(3):
        a, b = pairs[0][j], pairs[1][j]
        blocks.append(jnp.where(row < 12, a, turned(b, 12)))
        blocks.append(jnp.where(row < 12, turned(a, 12), b))
    return blocks


def blocks_of(value, n):
    return [value[72 * n + COLS * i : 72 * n + COLS * (i + 1)] for i in range(HALF)]


def set_bias(bias):
    last = (lax.axis_index("lat") == LAST_BAND).astype(jnp.int32)
    shape = (SPAN, SPAN)
    for s in range(2):
        labels = []
        for dim in range(2):
            i = lax.broadcasted_iota(jnp.int32, shape, dim)
            if s == 0:
                lat_row = i // COLS
                level = (i % COLS) // 12
            else:
                t = i % 72
                u = t % COLS
                lat_row = 2 * (t // COLS) + u // 12
                level = (u % 12) // 6
            labels.append((last * (lat_row < HALF).astype(jnp.int32), level))
        (kr, kl), (qr, ql) = labels
        same_row = kr == qr
        bias[s, 0] = jnp.where(same_row, 0.0, MASKED).astype(f32)
        bias[s, 1] = jnp.where(same_row & (kl == ql), 0.0, MASKED).astype(f32)


def norm_block(x, gain):
    mean = jnp.mean(x, axis=-1, keepdims=True)
    centered = x - mean
    inverse = lax.rsqrt(jnp.mean(centered * centered, axis=-1, keepdims=True) + 1e-05)
    xhat = centered * inverse
    return xhat, inverse, (xhat * gain).astype(bf16)


def load_windows(s, chunk_ref, gain_ref, normed, grads, xhat_ref, inverse_ref):
    gain = gain_ref[...]
    base = 2 * SPAN * s

    def store(off, xs, gs):
        x = jnp.concatenate(xs, axis=0)
        xhat, inverse, n = norm_block(x, gain)
        xhat_ref[base + off : base + off + 48] = xhat
        inverse_ref[base + off : base + off + 48] = jnp.broadcast_to(inverse, (48, LANES))
        normed[base + off : base + off + 48] = n
        grads[base + off : base + off + 48] = jnp.concatenate(gs, axis=0).astype(bf16)

    if s == 0:
        for p in range(2):
            halves = [chunk_ref(h, p)[...].astype(f32) for h in range(2)]
            xs = sum((blocks_of(v, 0) for v in halves), [])
            gs = sum((blocks_of(v, 1) for v in halves), [])
            for j in range(3):
                store(SPAN * p + 48 * j, xs[2 * j : 2 * j + 2], gs[2 * j : 2 * j + 2])
    else:
        parts = []
        for n in range(2):
            sides = []
            for kind in (2, 3):
                halves = [chunk_ref(h, kind)[...].astype(f32) for h in range(2)]
                sides.append(by_pair(sum((blocks_of(v, n) for v in halves), [])))
            parts.append([sides[0][p] + sides[1][p] for p in range(2)])
        for p in range(2):
            for j in range(3):
                store(
                    SPAN * p + 48 * j,
                    parts[0][p][2 * j : 2 * j + 2],
                    parts[1][p][2 * j : 2 * j + 2],
                )


def head_pair(s, p, lanes_of, bias, qkv, d_attn, attn, d_qkv):
    rows = slice(SPAN * p, SPAN * (p + 1))
    base = 2 * SPAN * s + SPAN * p
    out_rows = slice(base, base + SPAN)
    q = qkv[rows, lanes_of(0)]
    k = qkv[rows, lanes_of(1)]
    v = qkv[rows, lanes_of(2)]
    g = d_attn[rows, lanes_of(0)]
    lane = lax.broadcasted_iota(jnp.int32, (SPAN, LANES), 1)
    o, dq, dk, dv = [], [], [], []
    for e in range(2):
        mine = (lane < HEAD_DIM) if e == 0 else (lane >= HEAD_DIM)
        zero = jnp.zeros((), bf16)
        qm = jnp.where(mine, q, zero)
        km = jnp.where(mine, k, zero)
        vm = jnp.where(mine, v, zero)
        gm = jnp.where(mine, g, zero)
        scores = nt(k, qm) * (SCALE * LOG2E) + bias[s, p]
        top = jnp.max(scores, axis=0, keepdims=True)
        expo = jnp.exp2(scores - top)
        probs = expo * (1.0 / jnp.sum(expo, axis=0, keepdims=True))
        probs_b = probs.astype(bf16)
        d_probs = nt(v, gm)
        mean = jnp.sum(d_probs * probs, axis=0, keepdims=True)
        d_scores = (probs * (d_probs - mean) * SCALE).astype(bf16)
        o.append(tn(probs_b, vm))
        dv.append(nn(probs_b, gm))
        dq.append(tn(d_scores, km))
        dk.append(nn(d_scores, qm))
    attn[out_rows, lanes_of(0)] = (o[0] + o[1]).astype(bf16)
    d_qkv[out_rows, lanes_of(0)] = (dq[0] + dq[1]).astype(bf16)
    d_qkv[out_rows, lanes_of(1)] = (dk[0] + dk[1]).astype(bf16)
    d_qkv[out_rows, lanes_of(2)] = (dv[0] + dv[1]).astype(bf16)


def windows_front(s, chunk_ref, w, scratch):
    w_qkv, w_out, gain_ref = w
    (normed, grads, attn, d_qkv, qkv, d_attn, xhat_ref, inverse_ref, branch, shifted, bias, gain_sum) = scratch
    base = 2 * SPAN * s
    rows = slice(base, base + 2 * SPAN)
    load_windows(s, chunk_ref, gain_ref, normed, grads, xhat_ref, inverse_ref)
    for n in range(3):
        cols = slice(CH * n, CH * (n + 1))
        qkv[:, cols] = nn(normed[rows], w_qkv[:, cols]).astype(bf16)
    d_attn[...] = nt(grads[rows], w_out[...]).astype(bf16)

    def pair_step(hp, _):
        def lanes_of(n):
            return pl.ds(pl.multiple_of(CH * n + LANES * hp, LANES), LANES)

        for p in range(2):
            head_pair(s, p, lanes_of, bias, qkv, d_attn, attn, d_qkv)
        return 0

    lax.fori_loop(0, HEADS // 2, pair_step, 0)


def windows_back(s, result_ref, w, scratch):
    w_qkv, w_out, gain_ref = w
    (normed, grads, attn, d_qkv, qkv, d_attn, xhat_ref, inverse_ref, branch, shifted, bias, gain_sum) = scratch
    base = 2 * SPAN * s
    rows = slice(base, base + 2 * SPAN)
    branch[...] = nn(attn[rows], w_out[...])
    shifted[...] = nt(d_qkv[rows], w_qkv[...])
    gain = gain_ref[...]
    for i in range(6):
        at = slice(48 * i, 48 * (i + 1))
        there = slice(base + 48 * i, base + 48 * (i + 1))
        d_normed = shifted[at]
        xhat = xhat_ref[there]
        gain_sum[...] += jnp.sum((d_normed * xhat).reshape(6, 8, CH), axis=0)
        d_xhat = d_normed * gain
        mean = jnp.mean(d_xhat, axis=-1, keepdims=True)
        slope = jnp.mean(d_xhat * xhat, axis=-1, keepdims=True)
        shifted[at] = inverse_ref[there, 0:1] * (d_xhat - mean - xhat * slope)
    if s == 0:
        for p in range(2):
            for h in range(2):
                at = slice(SPAN * p + 72 * h, SPAN * p + 72 * (h + 1))
                result_ref(h, p)[...] = jnp.concatenate(
                    [branch[at], shifted[at]], axis=0
                ).astype(bf16)
    else:
        for side, kind in enumerate((2, 3)):
            blocks = []
            for value in (branch, shifted):
                pairs = [
                    [
                        value[SPAN * p + 72 * side + COLS * j : SPAN * p + 72 * side + COLS * (j + 1)]
                        for j in range(3)
                    ]
                    for p in range(2)
                ]
                blocks.append(by_row(pairs))
            for h in range(2):
                result_ref(h, kind)[...] = jnp.concatenate(
                    blocks[0][HALF * h : HALF * h + HALF] + blocks[1][HALF * h : HALF * h + HALF],
                    axis=0,
                ).astype(bf16)


def weight_grads(n, total, scratch):
    normed, grads, attn, d_qkv = scratch[:4]
    cols = slice(CH * n, CH * (n + 1))
    if n < 3:
        total[:, cols] = tn(normed[...], d_qkv[:, cols]).astype(bf16)
    else:
        total[:, cols] = tn(attn[...], grads[...]).astype(bf16)


def gain_rows(gain_sum, gain_out):
    row = jnp.sum(gain_sum[...], axis=0, keepdims=True)
    gain_out[...] = jnp.concatenate(
        [row[:, LANES * i : LANES * (i + 1)] for i in range(4)] + [jnp.zeros((4, LANES), f32)],
        axis=0,
    )


WINDOW_SCRATCH = [
    pltpu.VMEM((4 * SPAN, CH), bf16),
    pltpu.VMEM((4 * SPAN, CH), bf16),
    pltpu.VMEM((4 * SPAN, CH), bf16),
    pltpu.VMEM((4 * SPAN, 3 * CH), bf16),
    pltpu.VMEM((2 * SPAN, 3 * CH), bf16),
    pltpu.VMEM((2 * SPAN, CH), bf16),
    pltpu.VMEM((4 * SPAN, CH), f32),
    pltpu.VMEM((4 * SPAN, LANES), f32),
    pltpu.VMEM((2 * SPAN, CH), f32),
    pltpu.VMEM((2 * SPAN, CH), f32),
    pltpu.VMEM((2, 2, SPAN, SPAN), f32),
    pltpu.VMEM((8, CH), f32),
]


ORDER = (3, 0, 1, 2)
DIMS = (("x", "y"), ("y", "x"), ("x", "y"), ("y", "x"))


def partners():
    return (
        [along("core", 0)]
        + [along("x", k) for k in (1, 2, 3)]
        + [along("y", k) for k in (1, 2, 3)]
        + [along("z", k) for k in range(1, 8)]
    )


SUM_SCRATCH = [
    pltpu.VMEM((CH, GRADS), bf16),
    pltpu.VMEM((CH, GRADS), bf16),
    pltpu.VMEM((8, LANES), f32),
    pltpu.VMEM((256, GRADS), bf16),
    pltpu.VMEM((256, GRADS), bf16),
    pltpu.VMEM((4, 3, 64, CH), bf16),
    pltpu.VMEM((4, 64, CH), bf16),
    pltpu.VMEM((4, 3, 16, CH), bf16),
    pltpu.VMEM((2, 8, 16, 2 * CH), bf16),
    pltpu.VMEM((4, 8, 8, LANES), f32),
    pltpu.SemaphoreType.DMA((2, 4)),
    pltpu.SemaphoreType.DMA((2, 12)),
    pltpu.SemaphoreType.DMA((2, 12)),
    pltpu.SemaphoreType.DMA((2, 14)),
    pltpu.SemaphoreType.DMA((2, 14)),
    pltpu.SemaphoreType.DMA((2, 12)),
    pltpu.SemaphoreType.DMA((2, 12)),
    pltpu.SemaphoreType.DMA((2, 4)),
]


def ds(start, size):
    return pl.ds(pl.multiple_of(start, size), size)


class Sums:
    def __init__(self, gain_out, scratch):
        (self.total, self.out, self.gain_in, self.r0, self.b1, self.r1, self.b2, self.r2, self.zs, self.gs) = scratch[:10]
        sems = [(s.at[0], s.at[1]) for s in scratch[10:]]
        (self.s0, self.s1, self.s2, self.s3, self.sg, self.t2, self.t1, self.t0) = sems
        self.gain_out = gain_out
        x, y, z, core = place()
        self.at = {"x": x, "y": y, "z": z, "core": core}
        self.core = core
        self.started = []

    def go(self, copy):
        copy.start()
        self.started.append(copy)
        return copy

    def cols(self, j):
        n = ORDER[j]
        return slice(CH * n, CH * (n + 1))

    def core_send(self, j):
        cols = self.cols(j)
        theirs = ds((1 - self.core) * 256, 256)
        return self.go(
            send(self.total.at[theirs, cols], self.r0.at[:, cols], self.s0, j, along("core", 0))
        )

    def core_add(self, j):
        cols = self.cols(j)

        def step(i, _):
            here = ds(i * 64, 64)
            mine = ds(self.core * 256 + i * 64, 64)
            self.b1[here, cols] = (
                self.total[mine, cols].astype(f32) + self.r0[here, cols].astype(f32)
            ).astype(bf16)
            return 0

        lax.fori_loop(0, 4, step, 0)

    def first_send(self, j):
        d = DIMS[j][0]
        return [
            self.go(
                send(
                    self.b1.at[ds((self.at[d] + k) % 4 * 64, 64), self.cols(j)],
                    self.r1.at[j, k - 1],
                    self.s1,
                    3 * j + k - 1,
                    along(d, k),
                )
            )
            for k in (2, 1, 3)
        ]

    def first_add(self, j):
        d = DIMS[j][0]

        def step(i, _):
            here = ds(i * 16, 16)
            mine = ds(self.at[d] * 64 + i * 16, 16)
            total = self.b1[mine, self.cols(j)].astype(f32)
            for k in range(3):
                total += self.r1[j, k, here].astype(f32)
            self.b2[j, here] = total.astype(bf16)
            return 0

        lax.fori_loop(0, 4, step, 0)

    def second_send(self, j):
        d = DIMS[j][1]
        return [
            self.go(
                send(
                    self.b2.at[j, ds((self.at[d] + k) % 4 * 16, 16)],
                    self.r2.at[j, k - 1],
                    self.s2,
                    3 * j + k - 1,
                    along(d, k),
                )
            )
            for k in (2, 1, 3)
        ]

    def second_add(self, j):
        mine = ds(self.at[DIMS[j][1]] * 16, 16)
        total = self.b2[j, mine].astype(f32)
        for k in range(3):
            total += self.r2[j, k].astype(f32)
        cols = slice(CH * (j % 2), CH * (j % 2 + 1))
        self.zs[j // 2, self.at["z"], :, cols] = total.astype(bf16)

    def third_send(self, g):
        here = self.zs.at[g, self.at["z"]]
        return [
            self.go(send(here, here, self.s3, 7 * g + k - 1, along("z", k)))
            for k in (4, 3, 5, 2, 6, 1, 7)
        ]

    def rows(self, j, depth):
        start = self.core * 256
        if depth >= 1:
            start = start + self.at[DIMS[j][0]] * 64
        if depth >= 2:
            start = start + self.at[DIMS[j][1]] * 16
        return ds(start, (256, 64, 16)[depth])

    def third_add(self, g):
        total = self.zs[g, 0].astype(f32)
        for z in range(1, 8):
            total += self.zs[g, z].astype(f32)
        total = total.astype(bf16)
        for i in range(2):
            j = 2 * g + i
            self.out[self.rows(j, 2), self.cols(j)] = total[:, CH * i : CH * (i + 1)]

    def spread(self, j, depth):
        here = self.out.at[self.rows(j, depth), self.cols(j)]
        if depth == 0:
            return [self.go(send(here, here, self.t0, j, along("core", 0)))]
        d, sems = DIMS[j][depth - 1], (self.t1, self.t2)[depth - 1]
        return [self.go(send(here, here, sems, 3 * j + k - 1, along(d, k))) for k in (2, 1, 3)]

    def gain_send(self, stage):
        dim, size, first = (("core", 2, 0), ("x", 4, 1), ("y", 4, 4), ("z", 8, 7))[stage]
        here = self.gs.at[stage, self.at[dim]]
        return [
            self.go(send(here, here, self.sg, first + k - 1, along(dim, k)))
            for k in range(1, size)
        ]

    def gain_add(self, stage, copies):
        for copy in copies:
            copy.wait_recv()
        total = self.gs[stage, 0]
        for i in range(1, (2, 4, 4, 8)[stage]):
            total = total + self.gs[stage, i]
        if stage == 3:
            self.gain_out[...] = total
        else:
            self.gs[stage + 1, self.at["xyz"[stage]]] = total


def arrived(copies):
    for copy in copies:
        copy.wait_recv()


ROUTES = ((0, 0, 1, 0), (0, 1, 1, 0), (0, 2, 1, 0), (0, 3, 1, 1), (1, 3, 0, 1))


def halo_neighbours():
    return [neighbour(s * a, s * b) for s in (1, -1) for a, b in ((1, 0), (0, 1), (1, 1))]


def layer_kernel(
    tokens_hbm, cotangent_hbm, w_qkv_hbm, w_out_hbm, gain,
    layer_out, grad_tokens, grad_qkv, grad_out, gain_out,
    packed, work, result, back, tokens, cotangent, layer_buf, grad_buf, w_qkv, w_out,
    in_sems, out_sems, copy_sems, *scratch,
):
    window_scratch, sum_scratch = scratch[: len(WINDOW_SCRATCH)], scratch[len(WINDOW_SCRATCH) :]
    tokens_in = []
    for h in range(2):
        rows = slice(HALF * h, HALF * (h + 1))
        for n, (src, dst) in enumerate(((tokens_hbm, tokens), (cotangent_hbm, cotangent))):
            tokens_in.append(
                pltpu.make_async_copy(src.at[:, rows], dst.at[:, rows], copy_sems.at[8 + 2 * h + n])
            )
            tokens_in[-1].start()
    weights_in = [
        pltpu.make_async_copy(w_qkv_hbm, w_qkv, copy_sems.at[0]),
        pltpu.make_async_copy(w_out_hbm, w_out, copy_sems.at[1]),
    ]
    for copy in weights_in:
        copy.start()
    greeted = halo_neighbours() + partners()
    greet(greeted)
    for copy in tokens_in[:2]:
        copy.wait()
    pack_half(0, tokens, cotangent, packed)
    pl.semaphore_wait(pltpu.get_barrier_semaphore(), len(greeted))
    inward = []
    for n, (h, kind, a, b) in enumerate(ROUTES):
        if n == 4:
            for copy in tokens_in[2:]:
                copy.wait()
            pack_half(1, tokens, cotangent, packed)
        copy = send(
            packed.at[h, kind], work.at[n], (in_sems.at[0], in_sems.at[1]), n, neighbour(-a, -b)
        )
        copy.start()
        inward.append(copy)

    def chunk_ref(h, kind):
        if h == 1 and kind < 3:
            return packed.at[1, kind]
        return work.at[4 if h == 1 else kind]

    sums = Sums(gain_out, sum_scratch)
    set_bias(window_scratch[10])
    window_scratch[11][...] = jnp.zeros((8, CH), f32)
    w = (w_qkv, w_out, gain)
    for copy in weights_in:
        copy.wait()
    arrived(inward[0:2])
    windows_front(0, chunk_ref, w, window_scratch)
    arrived(inward[2:5])
    windows_front(1, chunk_ref, w, window_scratch)

    by_core, first, second, third, spread2, spread1, spread0 = {}, {}, {}, {}, {}, {}, {}
    for j in range(4):
        weight_grads(ORDER[j], sums.total, window_scratch)
        by_core[j] = sums.core_send(j)
        if j >= 1:
            by_core[j - 1].wait_recv()
            sums.core_add(j - 1)
            first[j - 1] = sums.first_send(j - 1)
    by_core[3].wait_recv()
    sums.core_add(3)
    first[3] = sums.first_send(3)

    for s in range(2):
        windows_back(s, lambda h, kind: result.at[h, kind], w, window_scratch)
    gain_rows(window_scratch[11], sums.gain_in)
    sums.gs[0, sums.core] = sums.gain_in[...]
    by_gain = sums.gain_send(0)
    for j in range(4):
        arrived(first[j])
        sums.first_add(j)
        second[j] = sums.second_send(j)
    outward = []
    for n, (h, kind, a, b) in enumerate(ROUTES):
        copy = send(
            result.at[h, kind], back.at[n], (out_sems.at[0], out_sems.at[1]), n, neighbour(a, b)
        )
        copy.start()
        outward.append(copy)
    sums.gain_add(0, by_gain)
    by_gain = sums.gain_send(1)
    for g in range(2):
        for j in (2 * g, 2 * g + 1):
            arrived(second[j])
            sums.second_add(j)
        third[g] = sums.third_send(g)
    sums.gain_add(1, by_gain)
    by_gain = sums.gain_send(2)
    for g in range(2):
        arrived(third[g])
        sums.third_add(g)
        for j in (2 * g, 2 * g + 1):
            spread2[j] = sums.spread(j, 2)
    sums.gain_add(2, by_gain)
    by_gain = sums.gain_send(3)

    arrived(outward)
    unpack_half(0, [back.at[n] for n in range(4)], tokens, cotangent, layer_buf, grad_buf)
    unpack_half(
        1,
        [result.at[1, kind] for kind in range(3)] + [back.at[4]],
        tokens,
        cotangent,
        layer_buf,
        grad_buf,
    )
    outputs = [
        pltpu.make_async_copy(layer_buf, layer_out, copy_sems.at[2]),
        pltpu.make_async_copy(grad_buf, grad_tokens, copy_sems.at[3]),
    ]
    for copy in outputs:
        copy.start()

    for j in range(4):
        arrived(spread2[j])
        spread1[j] = sums.spread(j, 1)
    sums.gain_add(3, by_gain)
    for j in range(4):
        arrived(spread1[j])
        spread0[j] = sums.spread(j, 0)
    for j in range(4):
        arrived(spread0[j])
        n = ORDER[j]
        cols = slice(CH * n, CH * (n + 1))
        outputs.append(
            pltpu.make_async_copy(
                sums.out.at[:, cols],
                grad_qkv.at[:, cols] if n < 3 else grad_out,
                copy_sems.at[4 + j],
            )
        )
        outputs[-1].start()
    for copy in inward + outward + sums.started:
        copy.wait_send()
    for copy in outputs:
        copy.wait()


VMEM = pl.BlockSpec(memory_space=pltpu.VMEM)
ANY = pl.BlockSpec(memory_space=pl.ANY)
LIMIT = 60 * 1024 * 1024


def local(tokens, cotangent, w_qkv, w_out, norm_gain_vector):
    shape = jax.ShapeDtypeStruct
    layer_out, grad_tokens, grad_qkv, grad_out, gain_out = pl.pallas_call(
        layer_kernel,
        out_shape=(
            shape(tokens.shape, bf16),
            shape(tokens.shape, bf16),
            shape((CH, 3 * CH), bf16),
            shape((CH, CH), bf16),
            shape((8, LANES), f32),
        ),
        in_specs=[ANY, ANY, ANY, ANY, VMEM],
        out_specs=(ANY, ANY, ANY, ANY, VMEM),
        scratch_shapes=[
            pltpu.VMEM((2, 4, CHUNK, CH), bf16),
            pltpu.VMEM((5, CHUNK, CH), bf16),
            pltpu.VMEM((2, 4, CHUNK, CH), bf16),
            pltpu.VMEM((5, CHUNK, CH), bf16),
            pltpu.VMEM(tokens.shape, bf16),
            pltpu.VMEM(tokens.shape, bf16),
            pltpu.VMEM(tokens.shape, bf16),
            pltpu.VMEM(tokens.shape, bf16),
            pltpu.VMEM((CH, 3 * CH), bf16),
            pltpu.VMEM((CH, CH), bf16),
            pltpu.SemaphoreType.DMA((2, 5)),
            pltpu.SemaphoreType.DMA((2, 5)),
            pltpu.SemaphoreType.DMA((12,)),
        ]
        + WINDOW_SCRATCH
        + SUM_SCRATCH,
        compiler_params=pltpu.CompilerParams(
            collective_id=0, has_side_effects=True, vmem_limit_bytes=LIMIT
        ),
    )(tokens, cotangent, w_qkv, w_out, norm_gain_vector.reshape(1, CH))
    return (layer_out, grad_tokens, grad_qkv, grad_out, gain_out[:4].reshape(CH))


def solution(mesh):
    return jax.shard_map(
        local,
        mesh=mesh,
        in_specs=(P(None, "lat", "lon", None), P(None, "lat", "lon", None), P(), P(), P()),
        out_specs=(P(None, "lat", "lon", None), P(None, "lat", "lon", None), P(), P(), P()),
        check_vma=False,
    )
```

time: 112 us -> 88.8 us (0.79)
  Pallas kernels: 104 us -> 80.5 us
    pallas_call x3 -> x1, Pallas kernels: 104 us -> 80.5 us  [local(): pl.pallas_call(layer_kernel, out_shape=(shape(tokens.shape, bf16), shape(...]
    slice x2 -> x0, local copies, waits for them, and re-layouts: 4.61 us -> none  [the longest x1 2.75 us: local(): out[:, :3 * CH]]
    unnamed x6 -> x8, local copies, waits for them, and re-layouts: 1.64 us -> 6.04 us
where the time goes in v2:
time: 88.8 us; the launch traced here: 88.6 us
  Pallas kernels  80.5 us (91%)
  local copies, waits for them, and re-layouts  7.41 us (8%)
    pallas_call x1, Pallas kernels, local(): pl.pallas_call(layer_kernel, out_shape=(shape(tokens.shape, bf16), shape(...  80.5 us
    unnamed x8, local copies, waits for them, and re-layouts  6.04 us

profile of v2, /device:TPU:1, one launch (start us, length us, event | category | flops | bytes accessed | tf_op | source)
XLA Modules:
  0.0 88.6 jit_solution(1571607868864130571)
XLA Ops:
  0.6 80.5 %shard_map.92 = (bf16[4,6,24,512]{3,2,1,0:T(8,128)(2,1)}, bf16[4,6,24,512]{3,2,1,0:T(8,128)(2,1)}, bf16[512,1536]{1,0:T(8,128)(2,1)}, bf16[512,512]{1,0:T(8,128)(2,1)}, f32[8,128]{1,0:T(8,128)}) custom-call(bf16[4,6,24,512]{3,2,1,0:T(8,128)(2,1)} %tokens_hbm.1, bf16[4,6,24,512]{3,2,1,0:T(8,128)(2,1)} %cotangent_hbm.1, bf16[512,1536]{1,0:T(8,128)(2,1)} %w_qkv_hbm.1, ...), custom_call_target="tpu_custom_call" | custom-call | tf_op jit(solution)/shard_map/pallas_call | solution.py:721
  81.1 0.0 copy-start
  81.1 1.4 %slice_bitcast_fusion = f32[512]{0:T(512)} fusion(f32[8,128]{1,0:T(8,128)} %get-tuple-element.14), kind=kLoop, calls=%fused_computation | loop fusion | bytes 4096 | tf_op jit(solution)/shard_map/reshape | solution.py:753
  82.5 1.9 %copy.14 = bf16[4,6,24,512]{3,2,1,0:T(8,128)(2,1)} copy(bf16[4,6,24,512]{3,2,1,0:T(8,128)(2,1)} %get-tuple-element.20) | data formatting | bytes 1179648
  84.4 1.9 %copy.15 = bf16[4,6,24,512]{3,2,1,0:T(8,128)(2,1)} copy(bf16[4,6,24,512]{3,2,1,0:T(8,128)(2,1)} %get-tuple-element.21) | data formatting | bytes 1179648
  86.4 0.0 copy-done
  86.4 0.0 copy-start.1
  86.4 1.1 %copy.16 = bf16[512,1536]{1,0:T(8,128)(2,1)} copy(bf16[512,1536]{1,0:T(8,128)(2,1)S(1)} %copy-done) | data formatting | bytes 3145728
  87.5 0.3 copy-done.1
  87.8 0.8 copy.17
Async XLA Ops:
  81.1 5.2 %copy-start = (bf16[512,1536]{1,0:T(8,128)(2,1)S(1)}, bf16[512,1536]{1,0:T(8,128)(2,1)}, u32[]{:S(2)}) copy-start(bf16[512,1536]{1,0:T(8,128)(2,1)} %get-tuple-element.22) | copy-start | bytes 4718596
  86.4 1.4 %copy-start.1 = (bf16[512,512]{1,0:T(8,128)(2,1)S(1)}, bf16[512,512]{1,0:T(8,128)(2,1)}, u32[]{:S(2)}) copy-start(bf16[512,512]{1,0:T(8,128)(2,1)} %get-tuple-element.23) | copy-start | bytes 1572868

commit v3 on v2

--- a/solution.py
+++ b/solution.py
@@ -22,6 +22,8 @@
 LOG2E = 1.4426950408889634
 MASKED = -1e30
 LANES = 128
+GROUP = 4
+GROUP_LANES = GROUP * HEAD_DIM
 MESH = pl.DeviceIdType.MESH
 f32 = jnp.float32
 bf16 = jnp.bfloat16
@@ -177,11 +179,11 @@
 
 def set_bias(bias):
     last = (lax.axis_index("lat") == LAST_BAND).astype(jnp.int32)
-    shape = (SPAN, SPAN)
+    shape = (SPAN, GROUP * SPAN)
     for s in range(2):
         labels = []
         for dim in range(2):
-            i = lax.broadcasted_iota(jnp.int32, shape, dim)
+            i = lax.broadcasted_iota(jnp.int32, shape, dim) % SPAN
             if s == 0:
                 lat_row = i // COLS
                 level = (i % COLS) // 12
@@ -241,39 +243,41 @@
                 )
 
 
-def head_pair(s, p, lanes_of, bias, qkv, d_attn, attn, d_qkv):
+def head_group(s, p, i, bias, qkv, d_attn, attn, d_qkv):
     rows = slice(SPAN * p, SPAN * (p + 1))
     base = 2 * SPAN * s + SPAN * p
     out_rows = slice(base, base + SPAN)
-    q = qkv[rows, lanes_of(0)]
-    k = qkv[rows, lanes_of(1)]
-    v = qkv[rows, lanes_of(2)]
-    g = d_attn[rows, lanes_of(0)]
-    lane = lax.broadcasted_iota(jnp.int32, (SPAN, LANES), 1)
-    o, dq, dk, dv = [], [], [], []
-    for e in range(2):
-        mine = (lane < HEAD_DIM) if e == 0 else (lane >= HEAD_DIM)
-        zero = jnp.zeros((), bf16)
-        qm = jnp.where(mine, q, zero)
-        km = jnp.where(mine, k, zero)
-        vm = jnp.where(mine, v, zero)
-        gm = jnp.where(mine, g, zero)
-        scores = nt(k, qm) * (SCALE * LOG2E) + bias[s, p]
-        top = jnp.max(scores, axis=0, keepdims=True)
-        expo = jnp.exp2(scores - top)
-        probs = expo * (1.0 / jnp.sum(expo, axis=0, keepdims=True))
-        probs_b = probs.astype(bf16)
-        d_probs = nt(v, gm)
-        mean = jnp.sum(d_probs * probs, axis=0, keepdims=True)
-        d_scores = (probs * (d_probs - mean) * SCALE).astype(bf16)
-        o.append(tn(probs_b, vm))
-        dv.append(nn(probs_b, gm))
-        dq.append(tn(d_scores, km))
-        dk.append(nn(d_scores, qm))
-    attn[out_rows, lanes_of(0)] = (o[0] + o[1]).astype(bf16)
-    d_qkv[out_rows, lanes_of(0)] = (dq[0] + dq[1]).astype(bf16)
-    d_qkv[out_rows, lanes_of(1)] = (dk[0] + dk[1]).astype(bf16)
-    d_qkv[out_rows, lanes_of(2)] = (dv[0] + dv[1]).astype(bf16)
+
+    def lanes(n):
+        return slice(CH * n + GROUP_LANES * i, CH * n + GROUP_LANES * (i + 1))
+
+    q, k, v = (qkv[rows, lanes(n)] for n in range(3))
+    g = d_attn[rows, lanes(0)]
+    head = lax.broadcasted_iota(jnp.int32, (SPAN, GROUP_LANES), 1) // HEAD_DIM
+    zero = jnp.zeros((), bf16)
+
+    def split(a):
+        return jnp.concatenate([jnp.where(head == e, a, zero) for e in range(GROUP)], axis=0)
+
+    def join(a):
+        picked = a[:SPAN]
+        for e in range(1, GROUP):
+            picked = jnp.where(head == e, a[SPAN * e : SPAN * (e + 1)], picked)
+        return picked
+
+    qs, gs = split(q), split(g)
+    scores = nt(k, qs) * (SCALE * LOG2E) + bias[s, p]
+    top = jnp.max(scores, axis=0, keepdims=True)
+    expo = jnp.exp2(scores - top)
+    probs = expo * (1.0 / jnp.sum(expo, axis=0, keepdims=True))
+    probs_b = probs.astype(bf16)
+    d_probs = nt(v, gs)
+    mean = jnp.sum(d_probs * probs, axis=0, keepdims=True)
+    d_scores = (probs * (d_probs - mean)).astype(bf16)
+    attn[out_rows, lanes(0)] = join(tn(probs_b, v)).astype(bf16)
+    d_qkv[out_rows, lanes(0)] = (join(tn(d_scores, k)) * SCALE).astype(bf16)
+    d_qkv[out_rows, lanes(1)] = (nn(d_scores, qs) * SCALE).astype(bf16)
+    d_qkv[out_rows, lanes(2)] = nn(probs_b, gs).astype(bf16)
 
 
 def windows_front(s, chunk_ref, w, scratch):
@@ -287,15 +291,9 @@
         qkv[:, cols] = nn(normed[rows], w_qkv[:, cols]).astype(bf16)
     d_attn[...] = nt(grads[rows], w_out[...]).astype(bf16)
 
-    def pair_step(hp, _):
-        def lanes_of(n):
-            return pl.ds(pl.multiple_of(CH * n + LANES * hp, LANES), LANES)
-
+    for i in range(HEADS // GROUP):
         for p in range(2):
-            head_pair(s, p, lanes_of, bias, qkv, d_attn, attn, d_qkv)
-        return 0
-
-    lax.fori_loop(0, HEADS // 2, pair_step, 0)
+            head_group(s, p, i, bias, qkv, d_attn, attn, d_qkv)
 
 
 def windows_back(s, result_ref, w, scratch):
@@ -370,7 +368,7 @@
     pltpu.VMEM((4 * SPAN, LANES), f32),
     pltpu.VMEM((2 * SPAN, CH), f32),
     pltpu.VMEM((2 * SPAN, CH), f32),
-    pltpu.VMEM((2, 2, SPAN, SPAN), f32),
+    pltpu.VMEM((2, 2, SPAN, GROUP * SPAN), f32),
     pltpu.VMEM((8, CH), f32),
 ]
 
@@ -396,19 +394,22 @@
     pltpu.VMEM((256, GRADS), bf16),
     pltpu.VMEM((4, 3, 64, CH), bf16),
     pltpu.VMEM((4, 64, CH), bf16),
-    pltpu.VMEM((4, 3, 16, CH), bf16),
-    pltpu.VMEM((2, 8, 16, 2 * CH), bf16),
+    pltpu.VMEM((4, 7, 16, 256), bf16),
+    pltpu.VMEM((4, 4, 16, 256), bf16),
     pltpu.VMEM((4, 8, 8, LANES), f32),
     pltpu.SemaphoreType.DMA((2, 4)),
     pltpu.SemaphoreType.DMA((2, 12)),
+    pltpu.SemaphoreType.DMA((2, 28)),
     pltpu.SemaphoreType.DMA((2, 12)),
     pltpu.SemaphoreType.DMA((2, 14)),
-    pltpu.SemaphoreType.DMA((2, 14)),
-    pltpu.SemaphoreType.DMA((2, 12)),
+    pltpu.SemaphoreType.DMA((2, 28)),
     pltpu.SemaphoreType.DMA((2, 12)),
     pltpu.SemaphoreType.DMA((2, 4)),
 ]
 
+NEAR_LAST_4 = (2, 1, 3)
+NEAR_LAST_8 = (4, 3, 5, 2, 6, 1, 7)
+
 
 def ds(start, size):
     return pl.ds(pl.multiple_of(start, size), size)
@@ -416,7 +417,7 @@
 
 class Sums:
     def __init__(self, gain_out, scratch):
-        (self.total, self.out, self.gain_in, self.r0, self.b1, self.r1, self.b2, self.r2, self.zs, self.gs) = scratch[:10]
+        (self.total, self.out, self.gain_in, self.r0, self.b1, self.r1, self.b2, self.r2, self.ys, self.gs) = scratch[:10]
         sems = [(s.at[0], s.at[1]) for s in scratch[10:]]
         (self.s0, self.s1, self.s2, self.s3, self.sg, self.t2, self.t1, self.t0) = sems
         self.gain_out = gain_out
@@ -466,7 +467,7 @@
                     along(d, k),
                 )
             )
-            for k in (2, 1, 3)
+            for k in NEAR_LAST_4
         ]
 
     def first_add(self, j):
@@ -484,58 +485,54 @@
         lax.fori_loop(0, 4, step, 0)
 
     def second_send(self, j):
+        copies = []
+        for k in NEAR_LAST_8:
+            z = (self.at["z"] + k) % 8
+            src = self.b2.at[j, ds(z // 2 * 16, 16), ds(z % 2 * 256, 256)]
+            copies.append(
+                self.go(send(src, self.r2.at[j, k - 1], self.s2, 7 * j + k - 1, along("z", k)))
+            )
+        return copies
+
+    def second_add(self, j):
+        z = self.at["z"]
+        total = self.b2[j, ds(z // 2 * 16, 16), ds(z % 2 * 256, 256)].astype(f32)
+        for k in range(7):
+            total += self.r2[j, k].astype(f32)
+        self.ys[j, self.at[DIMS[j][1]]] = total.astype(bf16)
+
+    def third_send(self, j):
         d = DIMS[j][1]
+        here = self.ys.at[j, self.at[d]]
         return [
-            self.go(
-                send(
-                    self.b2.at[j, ds((self.at[d] + k) % 4 * 16, 16)],
-                    self.r2.at[j, k - 1],
-                    self.s2,
-                    3 * j + k - 1,
-                    along(d, k),
-                )
-            )
-            for k in (2, 1, 3)
+            self.go(send(here, here, self.s3, 3 * j + k - 1, along(d, k))) for k in NEAR_LAST_4
         ]
 
-    def second_add(self, j):
-        mine = ds(self.at[DIMS[j][1]] * 16, 16)
-        total = self.b2[j, mine].astype(f32)
-        for k in range(3):
-            total += self.r2[j, k].astype(f32)
-        cols = slice(CH * (j % 2), CH * (j % 2 + 1))
-        self.zs[j // 2, self.at["z"], :, cols] = total.astype(bf16)
-
-    def third_send(self, g):
-        here = self.zs.at[g, self.at["z"]]
-        return [
-            self.go(send(here, here, self.s3, 7 * g + k - 1, along("z", k)))
-            for k in (4, 3, 5, 2, 6, 1, 7)
-        ]
-
-    def rows(self, j, depth):
+    def piece(self, j, depth):
         start = self.core * 256
         if depth >= 1:
             start = start + self.at[DIMS[j][0]] * 64
-        if depth >= 2:
-            start = start + self.at[DIMS[j][1]] * 16
-        return ds(start, (256, 64, 16)[depth])
-
-    def third_add(self, g):
-        total = self.zs[g, 0].astype(f32)
-        for z in range(1, 8):
-            total += self.zs[g, z].astype(f32)
-        total = total.astype(bf16)
-        for i in range(2):
-            j = 2 * g + i
-            self.out[self.rows(j, 2), self.cols(j)] = total[:, CH * i : CH * (i + 1)]
+        if depth < 2:
+            return ds(start, (256, 64)[depth]), self.cols(j)
+        z = self.at["z"]
+        return ds(start + z // 2 * 16, 16), ds(CH * ORDER[j] + z % 2 * 256, 256)
+
+    def third_add(self, j):
+        total = self.ys[j, 0].astype(f32)
+        for i in range(1, 4):
+            total += self.ys[j, i].astype(f32)
+        rows, cols = self.piece(j, 2)
+        self.out[rows, cols] = total.astype(bf16)
 
     def spread(self, j, depth):
-        here = self.out.at[self.rows(j, depth), self.cols(j)]
-        if depth == 0:
-            return [self.go(send(here, here, self.t0, j, along("core", 0)))]
-        d, sems = DIMS[j][depth - 1], (self.t1, self.t2)[depth - 1]
-        return [self.go(send(here, here, sems, 3 * j + k - 1, along(d, k))) for k in (2, 1, 3)]
+        rows, cols = self.piece(j, depth)
+        here = self.out.at[rows, cols]
+        dim, sems, first, near_last = (
+            ("core", self.t0, j, (1,)),
+            (DIMS[j][0], self.t1, 3 * j, NEAR_LAST_4),
+            ("z", self.t2, 7 * j, NEAR_LAST_8),
+        )[depth]
+        return [self.go(send(here, here, sems, first + k - 1, along(dim, k))) for k in near_last]
 
     def gain_send(self, stage):
         dim, size, first = (("core", 2, 0), ("x", 4, 1), ("y", 4, 4), ("z", 8, 7))[stage]
@@ -619,8 +616,24 @@
     w = (w_qkv, w_out, gain)
     for copy in weights_in:
         copy.wait()
+    def result_ref(h, kind):
+        return result.at[h, kind]
+
+    outward = []
+
+    def send_back(numbers):
+        for n in numbers:
+            h, kind, a, b = ROUTES[n]
+            copy = send(
+                result.at[h, kind], back.at[n], (out_sems.at[0], out_sems.at[1]), n, neighbour(a, b)
+            )
+            copy.start()
+            outward.append(copy)
+
     arrived(inward[0:2])
     windows_front(0, chunk_ref, w, window_scratch)
+    windows_back(0, result_ref, w, window_scratch)
+    send_back((0, 1))
     arrived(inward[2:5])
     windows_front(1, chunk_ref, w, window_scratch)
 
@@ -636,8 +649,7 @@
     sums.core_add(3)
     first[3] = sums.first_send(3)
 
-    for s in range(2):
-        windows_back(s, lambda h, kind: result.at[h, kind], w, window_scratch)
+    windows_back(1, result_ref, w, window_scratch)
     gain_rows(window_scratch[11], sums.gain_in)
     sums.gs[0, sums.core] = sums.gain_in[...]
     by_gain = sums.gain_send(0)
@@ -645,46 +657,35 @@
         arrived(first[j])
         sums.first_add(j)
         second[j] = sums.second_send(j)
-    outward = []
-    for n, (h, kind, a, b) in enumerate(ROUTES):
-        copy = send(
-            result.at[h, kind], back.at[n], (out_sems.at[0], out_sems.at[1]), n, neighbour(a, b)
-        )
-        copy.start()
-        outward.append(copy)
+    send_back((3, 2, 4))
     sums.gain_add(0, by_gain)
     by_gain = sums.gain_send(1)
-    for g in range(2):
-        for j in (2 * g, 2 * g + 1):
-            arrived(second[j])
-            sums.second_add(j)
-        third[g] = sums.third_send(g)
+    for j in range(4):
+        arrived(second[j])
+        sums.second_add(j)
+        third[j] = sums.third_send(j)
     sums.gain_add(1, by_gain)
     by_gain = sums.gain_send(2)
-    for g in range(2):
-        arrived(third[g])
-        sums.third_add(g)
-        for j in (2 * g, 2 * g + 1):
-            spread2[j] = sums.spread(j, 2)
+    for j in range(4):
+        arrived(third[j])
+        sums.third_add(j)
+        spread2[j] = sums.spread(j, 2)
     sums.gain_add(2, by_gain)
     by_gain = sums.gain_send(3)
 
     arrived(outward)
-    unpack_half(0, [back.at[n] for n in range(4)], tokens, cotangent, layer_buf, grad_buf)
-    unpack_half(
-        1,
-        [result.at[1, kind] for kind in range(3)] + [back.at[4]],
-        tokens,
-        cotangent,
-        layer_buf,
-        grad_buf,
-    )
-    outputs = [
-        pltpu.make_async_copy(layer_buf, layer_out, copy_sems.at[2]),
-        pltpu.make_async_copy(grad_buf, grad_tokens, copy_sems.at[3]),
-    ]
-    for copy in outputs:
-        copy.start()
+    outputs = []
+    for h in range(2):
+        chunks = [back.at[n] for n in range(4)]
+        if h == 1:
+            chunks = [result.at[1, kind] for kind in range(3)] + [back.at[4]]
+        unpack_half(h, chunks, tokens, cotangent, layer_buf, grad_buf)
+        rows = slice(HALF * h, HALF * (h + 1))
+        for n, (src, dst) in enumerate(((layer_buf, layer_out), (grad_buf, grad_tokens))):
+            outputs.append(
+                pltpu.make_async_copy(src.at[:, rows], dst.at[:, rows], copy_sems.at[12 + 2 * h + n])
+            )
+            outputs[-1].start()
 
     for j in range(4):
         arrived(spread2[j])
@@ -711,23 +712,35 @@
         copy.wait()
 
 
+def publish_kernel(*refs):
+    inputs, outputs, sems = refs[:5], refs[5:10], refs[10]
+    copies = [pltpu.make_async_copy(inputs[n], outputs[n], sems.at[n]) for n in range(4)]
+    for copy in copies:
+        copy.start()
+    rows = inputs[4][...]
+    outputs[4][...] = jnp.concatenate([rows[i : i + 1] for i in range(4)], axis=1)
+    for copy in copies:
+        copy.wait()
+
+
 VMEM = pl.BlockSpec(memory_space=pltpu.VMEM)
 ANY = pl.BlockSpec(memory_space=pl.ANY)
+HBM = pl.BlockSpec(memory_space=pltpu.HBM)
 LIMIT = 60 * 1024 * 1024
 
 
 def local(tokens, cotangent, w_qkv, w_out, norm_gain_vector):
     shape = jax.ShapeDtypeStruct
-    layer_out, grad_tokens, grad_qkv, grad_out, gain_out = pl.pallas_call(
+    large = (
+        shape(tokens.shape, bf16),
+        shape(tokens.shape, bf16),
+        shape((CH, 3 * CH), bf16),
+        shape((CH, CH), bf16),
+    )
+    results = pl.pallas_call(
         layer_kernel,
-        out_shape=(
-            shape(tokens.shape, bf16),
-            shape(tokens.shape, bf16),
-            shape((CH, 3 * CH), bf16),
-            shape((CH, CH), bf16),
-            shape((8, LANES), f32),
-        ),
-        in_specs=[ANY, ANY, ANY, ANY, VMEM],
+        out_shape=large + (shape((8, LANES), f32),),
+        in_specs=[HBM, HBM, HBM, HBM, VMEM],
         out_specs=(ANY, ANY, ANY, ANY, VMEM),
         scratch_shapes=[
             pltpu.VMEM((2, 4, CHUNK, CH), bf16),
@@ -742,7 +755,7 @@
             pltpu.VMEM((CH, CH), bf16),
             pltpu.SemaphoreType.DMA((2, 5)),
             pltpu.SemaphoreType.DMA((2, 5)),
-            pltpu.SemaphoreType.DMA((12,)),
+            pltpu.SemaphoreType.DMA((16,)),
         ]
         + WINDOW_SCRATCH
         + SUM_SCRATCH,
@@ -750,7 +763,15 @@
             collective_id=0, has_side_effects=True, vmem_limit_bytes=LIMIT
         ),
     )(tokens, cotangent, w_qkv, w_out, norm_gain_vector.reshape(1, CH))
-    return (layer_out, grad_tokens, grad_qkv, grad_out, gain_out[:4].reshape(CH))
+    layer_out, grad_tokens, grad_qkv, grad_out, gain_out = pl.pallas_call(
+        publish_kernel,
+        out_shape=large + (shape((1, CH), f32),),
+        in_specs=[ANY, ANY, ANY, ANY, VMEM],
+        out_specs=(HBM, HBM, HBM, HBM, VMEM),
+        scratch_shapes=[pltpu.SemaphoreType.DMA((4,))],
+        compiler_params=pltpu.CompilerParams(vmem_limit_bytes=8 * 1024 * 1024),
+    )(*results)
+    return (layer_out, grad_tokens, grad_qkv, grad_out, gain_out.reshape(CH))
 
 
 def solution(mesh):

time: 88.8 us -> 77.7 us (0.88)
  Pallas kernels: 80.5 us -> 71.5 us
  local copies, waits for them, and re-layouts: 7.41 us -> 5.25 us
    pallas_call x1 -> x2, Pallas kernels: 80.5 us -> 71.5 us  [the longest x1 69.2 us: local(): pl.pallas_call(layer_kernel, out_shape=large + (shape((8, LANES), f32),),...]
    reshape x1 -> x0, local copies, waits for them, and re-layouts: 1.38 us -> none  [local(): gain_out[:4].reshape(CH)]
    unnamed x8 -> x10, local copies, waits for them, and re-layouts: 6.04 us -> 5.25 us
where the time goes in v3:
time: 77.7 us; the launch traced here: 77.4 us
  Pallas kernels  71.5 us (92%)
  local copies, waits for them, and re-layouts  5.25 us (7%)
    pallas_call x1, Pallas kernels, local(): pl.pallas_call(layer_kernel, out_shape=large + (shape((8, LANES), f32),),...  69.2 us
    unnamed x10, local copies, waits for them, and re-layouts  5.25 us
    pallas_call x1, Pallas kernels, local(): pl.pallas_call(publish_kernel, out_shape=large + (shape((1, CH), f32),),...  2.31 us

profile of v3, /device:TPU:1, one launch (start us, length us, event | category | flops | bytes accessed | tf_op | source)
XLA Modules:
  0.0 77.4 jit_solution(15081085303522985295)
XLA Ops:
  0.6 69.2 %shard_map.92 = (bf16[4,6,24,512]{3,2,1,0:T(8,128)(2,1)}, bf16[4,6,24,512]{3,2,1,0:T(8,128)(2,1)}, bf16[512,1536]{1,0:T(8,128)(2,1)}, bf16[512,512]{1,0:T(8,128)(2,1)}, f32[8,128]{1,0:T(8,128)}) custom-call(bf16[4,6,24,512]{3,2,1,0:T(8,128)(2,1)} %tokens_hbm.1, bf16[4,6,24,512]{3,2,1,0:T(8,128)(2,1)} %cotangent_hbm.1, bf16[512,1536]{1,0:T(8,128)(2,1)} %w_qkv_hbm.1, ...), custom_call_target="tpu_custom_call" | custom-call | tf_op jit(solution)/shard_map/pallas_call | solution.py:740
  69.8 0.0 copy-start
  69.8 1.4 %copy-done = bf16[512,1536]{1,0:T(8,128)(2,1)S(1)} copy-done((bf16[512,1536]{1,0:T(8,128)(2,1)S(1)}, bf16[512,1536]{1,0:T(8,128)(2,1)}, u32[]{:S(2)}) %copy-start) | copy-done | bytes 1572888
  71.2 0.0 copy-start.1
  71.2 1.1 %copy-done.1 = bf16[4,6,24,512]{3,2,1,0:T(8,128)(2,1)S(1)} copy-done((bf16[4,6,24,512]{3,2,1,0:T(8,128)(2,1)S(1)}, bf16[4,6,24,512]{3,2,1,0:T(8,128)(2,1)}, u32[]{:S(2)}) %copy-start.1) | copy-done | bytes 589848
  72.3 0.0 copy-start.2
  72.3 1.1 %copy-done.2 = bf16[4,6,24,512]{3,2,1,0:T(8,128)(2,1)S(1)} copy-done((bf16[4,6,24,512]{3,2,1,0:T(8,128)(2,1)S(1)}, bf16[4,6,24,512]{3,2,1,0:T(8,128)(2,1)}, u32[]{:S(2)}) %copy-start.2) | copy-done | bytes 589848
  73.4 0.0 copy-start.3
  73.4 1.0 %copy-done.3 = bf16[512,512]{1,0:T(8,128)(2,1)S(1)} copy-done((bf16[512,512]{1,0:T(8,128)(2,1)S(1)}, bf16[512,512]{1,0:T(8,128)(2,1)}, u32[]{:S(2)}) %copy-start.3) | copy-done | bytes 524312
  74.4 0.0 copy-start.4
  74.4 0.7 copy-done.4
  75.1 2.3 %shard_map.93 = (bf16[4,6,24,512]{3,2,1,0:T(8,128)(2,1)}, bf16[4,6,24,512]{3,2,1,0:T(8,128)(2,1)}, bf16[512,1536]{1,0:T(8,128)(2,1)}, bf16[512,512]{1,0:T(8,128)(2,1)}, f32[1,512]{1,0:T(1,128)}) custom-call(bf16[4,6,24,512]{3,2,1,0:T(8,128)(2,1)S(1)} %copy-done.1, bf16[4,6,24,512]{3,2,1,0:T(8,128)(2,1)S(1)} %copy-done.2, bf16[512,1536]{1,0:T(8,128)(2,1)S(1)} %copy-done, ...), custom_call_target="tpu_custom_call" | custom-call | tf_op jit(solution)/shard_map/pallas_call | solution.py:766
Async XLA Ops:
  69.8 1.4 %copy-start = (bf16[512,1536]{1,0:T(8,128)(2,1)S(1)}, bf16[512,1536]{1,0:T(8,128)(2,1)}, u32[]{:S(2)}) copy-start(bf16[512,1536]{1,0:T(8,128)(2,1)} %get-tuple-element.17.refs_2_) | copy-start | bytes 4718596
  71.2 1.1 %copy-start.1 = (bf16[4,6,24,512]{3,2,1,0:T(8,128)(2,1)S(1)}, bf16[4,6,24,512]{3,2,1,0:T(8,128)(2,1)}, u32[]{:S(2)}) copy-start(bf16[4,6,24,512]{3,2,1,0:T(8,128)(2,1)} %get-tuple-element.15.refs_0_) | copy-start | bytes 1769476
  72.3 1.1 %copy-start.2 = (bf16[4,6,24,512]{3,2,1,0:T(8,128)(2,1)S(1)}, bf16[4,6,24,512]{3,2,1,0:T(8,128)(2,1)}, u32[]{:S(2)}) copy-start(bf16[4,6,24,512]{3,2,1,0:T(8,128)(2,1)} %get-tuple-element.16.refs_1_) | copy-start | bytes 1769476
  73.4 1.0 %copy-start.3 = (bf16[512,512]{1,0:T(8,128)(2,1)S(1)}, bf16[512,512]{1,0:T(8,128)(2,1)}, u32[]{:S(2)}) copy-start(bf16[512,512]{1,0:T(8,128)(2,1)} %get-tuple-element.18.refs_3_) | copy-start | bytes 1572868
  74.4 0.7 copy-start.4

commit v4 on v3

--- a/solution.py
+++ b/solution.py
@@ -713,13 +713,17 @@
 
 
 def publish_kernel(*refs):
-    inputs, outputs, sems = refs[:5], refs[5:10], refs[10]
-    copies = [pltpu.make_async_copy(inputs[n], outputs[n], sems.at[n]) for n in range(4)]
-    for copy in copies:
+    inputs, outputs, bufs, sems = refs[:5], refs[5:10], refs[10:14], refs[14]
+    reads = [pltpu.make_async_copy(inputs[n], bufs[n], sems.at[0, n]) for n in range(4)]
+    writes = [pltpu.make_async_copy(bufs[n], outputs[n], sems.at[1, n]) for n in range(4)]
+    for copy in reads:
         copy.start()
     rows = inputs[4][...]
     outputs[4][...] = jnp.concatenate([rows[i : i + 1] for i in range(4)], axis=1)
-    for copy in copies:
+    for read, write in zip(reads, writes):
+        read.wait()
+        write.start()
+    for copy in writes:
         copy.wait()
 
 
@@ -768,8 +772,9 @@
         out_shape=large + (shape((1, CH), f32),),
         in_specs=[ANY, ANY, ANY, ANY, VMEM],
         out_specs=(HBM, HBM, HBM, HBM, VMEM),
-        scratch_shapes=[pltpu.SemaphoreType.DMA((4,))],
-        compiler_params=pltpu.CompilerParams(vmem_limit_bytes=8 * 1024 * 1024),
+        scratch_shapes=[pltpu.VMEM(a.shape, bf16) for a in large]
+        + [pltpu.SemaphoreType.DMA((2, 4))],
+        compiler_params=pltpu.CompilerParams(vmem_limit_bytes=LIMIT),
     )(*results)
     return (layer_out, grad_tokens, grad_qkv, grad_out, gain_out.reshape(CH))
 

time: 77.7 us -> 74.3 us (0.956)
  local copies, waits for them, and re-layouts: 5.25 us -> 0 us
  Pallas kernels: 71.5 us -> 73.6 us
    unnamed x10 -> x0, local copies, waits for them, and re-layouts: 5.25 us -> none
    pallas_call x1, Pallas kernels: 2.31 us -> 4.41 us  [local(): pl.pallas_call(publish_kernel, out_shape=large + (shape((1, CH), f32),),...]
where the time goes in v4:
time: 74.3 us; the launch traced here: 74.2 us
  Pallas kernels  73.6 us (99%)
    pallas_call x1, Pallas kernels, local(): pl.pallas_call(layer_kernel, out_shape=large + (shape((8, LANES), f32),),...  69.1 us
    pallas_call x1, Pallas kernels, local(): pl.pallas_call(publish_kernel, out_shape=large + (shape((1, CH), f32),),...  4.41 us

profile of v4, /device:TPU:1, one launch (start us, length us, event | category | flops | bytes accessed | tf_op | source)
XLA Modules:
  0.0 74.2 jit_solution(14863932090605044475)
XLA Ops:
  0.6 69.1 %shard_map.92 = (bf16[4,6,24,512]{3,2,1,0:T(8,128)(2,1)}, bf16[4,6,24,512]{3,2,1,0:T(8,128)(2,1)}, bf16[512,1536]{1,0:T(8,128)(2,1)}, bf16[512,512]{1,0:T(8,128)(2,1)}, f32[8,128]{1,0:T(8,128)}) custom-call(bf16[4,6,24,512]{3,2,1,0:T(8,128)(2,1)} %tokens_hbm.1, bf16[4,6,24,512]{3,2,1,0:T(8,128)(2,1)} %cotangent_hbm.1, bf16[512,1536]{1,0:T(8,128)(2,1)} %w_qkv_hbm.1, ...), custom_call_target="tpu_custom_call" | custom-call | tf_op jit(solution)/shard_map/pallas_call | solution.py:744
  69.8 4.4 %shard_map.93 = (bf16[4,6,24,512]{3,2,1,0:T(8,128)(2,1)}, bf16[4,6,24,512]{3,2,1,0:T(8,128)(2,1)}, bf16[512,1536]{1,0:T(8,128)(2,1)}, bf16[512,512]{1,0:T(8,128)(2,1)}, f32[1,512]{1,0:T(1,128)}) custom-call(bf16[4,6,24,512]{3,2,1,0:T(8,128)(2,1)} %get-tuple-element.15.refs_0_, bf16[4,6,24,512]{3,2,1,0:T(8,128)(2,1)} %get-tuple-element.16.refs_1_, ...), custom_call_target="tpu_custom_call" | custom-call | tf_op jit(solution)/shard_map/pallas_call | solution.py:770

commit v5 on v4

--- a/solution.py
+++ b/solution.py
@@ -657,13 +657,13 @@
         arrived(first[j])
         sums.first_add(j)
         second[j] = sums.second_send(j)
-    send_back((3, 2, 4))
     sums.gain_add(0, by_gain)
     by_gain = sums.gain_send(1)
     for j in range(4):
         arrived(second[j])
         sums.second_add(j)
         third[j] = sums.third_send(j)
+    send_back((3, 2, 4))
     sums.gain_add(1, by_gain)
     by_gain = sums.gain_send(2)
     for j in range(4):

time: 74.3 us -> 76.3 us (1.027)
  Pallas kernels: 73.6 us -> 75.5 us
    pallas_call x1, Pallas kernels: 69.1 us -> 71.1 us  [local(): pl.pallas_call(layer_kernel, out_shape=large + (shape((8, LANES), f32),),...]
where the time goes in v5:
time: 76.3 us; the launch traced here: 76.2 us
  Pallas kernels  75.5 us (99%)
    pallas_call x1, Pallas kernels, local(): pl.pallas_call(layer_kernel, out_shape=large + (shape((8, LANES), f32),),...  71.1 us
    pallas_call x1, Pallas kernels, local(): pl.pallas_call(publish_kernel, out_shape=large + (shape((1, CH), f32),),...  4.41 us

profile of v5, /device:TPU:1, one launch (start us, length us, event | category | flops | bytes accessed | tf_op | source)
XLA Modules:
  0.0 76.2 jit_solution(9006641350943563163)
XLA Ops:
  0.6 71.1 %shard_map.92 = (bf16[4,6,24,512]{3,2,1,0:T(8,128)(2,1)}, bf16[4,6,24,512]{3,2,1,0:T(8,128)(2,1)}, bf16[512,1536]{1,0:T(8,128)(2,1)}, bf16[512,512]{1,0:T(8,128)(2,1)}, f32[8,128]{1,0:T(8,128)}) custom-call(bf16[4,6,24,512]{3,2,1,0:T(8,128)(2,1)} %tokens_hbm.1, bf16[4,6,24,512]{3,2,1,0:T(8,128)(2,1)} %cotangent_hbm.1, bf16[512,1536]{1,0:T(8,128)(2,1)} %w_qkv_hbm.1, ...), custom_call_target="tpu_custom_call" | custom-call | tf_op jit(solution)/shard_map/pallas_call | solution.py:744
  71.8 4.4 %shard_map.93 = (bf16[4,6,24,512]{3,2,1,0:T(8,128)(2,1)}, bf16[4,6,24,512]{3,2,1,0:T(8,128)(2,1)}, bf16[512,1536]{1,0:T(8,128)(2,1)}, bf16[512,512]{1,0:T(8,128)(2,1)}, f32[1,512]{1,0:T(1,128)}) custom-call(bf16[4,6,24,512]{3,2,1,0:T(8,128)(2,1)} %get-tuple-element.15.refs_0_, bf16[4,6,24,512]{3,2,1,0:T(8,128)(2,1)} %get-tuple-element.16.refs_1_, ...), custom_call_target="tpu_custom_call" | custom-call | tf_op jit(solution)/shard_map/pallas_call | solution.py:770
